TPU v7x, 32 devices: a whole 2x2x4 slice. The times are simulated.
32 devices in a mesh: series: 8 (over z, x), tm: 4 (over y, core).
Axes of the slice: x: 2, y: 2, z: 4, core: 2. Of those that a mesh axis runs over, the one named last changes fastest.
Arguments:
- inputs: bfloat16 [24, 1344, 512], P('series', 'tm'), may hold values from -6 to 6
- cotangent: bfloat16 [24, 1344, 512], P('series', 'tm'), may hold values from -6 to 6
- horizon: int32 [24], P('series'), may hold values from 96 to 720, as said below
- down_a: bfloat16 [12, 512, 512], P(None, None, 'tm'), may hold values from -0.078125 to 0.078125
- down_b: bfloat16 [16, 512, 512], P(None, None, 'tm'), may hold values from -0.0625 to 0.0625
- up_a: bfloat16 [12, 512, 512], P(None, None, 'tm'), may hold values from -0.25 to 0.25
- up_b: bfloat16 [16, 512, 512], P(None, None, 'tm'), may hold values from -0.25 to 0.25
- iso_a: bfloat16 [112, 512, 512], P(None, None, 'tm'), may hold values from -0.03125 to 0.03125
- iso_b: bfloat16 [84, 512, 512], P(None, None, 'tm'), may hold values from -0.0390625 to 0.0390625
- merge: bfloat16 [2, 512, 512], P(None, None, 'tm'), may hold values from -0.1875 to 0.1875
- ffn_in: bfloat16 [512, 2048], P(None, 'tm'), may hold values from -0.25 to 0.25
- ffn_out: bfloat16 [2048, 512], P(None, 'tm'), may hold values from -0.125 to 0.125
- gain0: bfloat16 [512], P('tm'), may hold values from 0.099609375 to 1.8984375
- gain1: bfloat16 [512], P('tm'), may hold values from 0.099609375 to 1.8984375
- gain2: bfloat16 [512], P('tm'), may hold values from 0.099609375 to 1.8984375
- regress: bfloat16 [1344, 1344], P('tm'), may hold values from -0.15625 to 0.15625
Outputs:
- output: bfloat16 [24, 1344, 512], P('series', 'tm')
- input_grad: bfloat16 [24, 1344, 512], P('series', 'tm')
- grad_down_a: float32 [12, 512, 512], P(None, 'series', 'tm')
- grad_down_b: float32 [16, 512, 512], P(None, 'series', 'tm')
- grad_up_a: float32 [12, 512, 512], P(None, 'series', 'tm')
- grad_up_b: float32 [16, 512, 512], P(None, 'series', 'tm')
- grad_iso_a: float32 [112, 512, 512], P(None, 'series', 'tm')
- grad_iso_b: float32 [84, 512, 512], P(None, 'series', 'tm')
- grad_merge: float32 [2, 512, 512], P(None, None, 'tm')
- grad_ffn_in: float32 [512, 2048], P(None, 'tm')
- grad_ffn_out: float32 [2048, 512], P(None, 'tm')
- grad_gain0: float32 [512], P('tm')
- grad_gain1: float32 [512], P('tm')
- grad_gain2: float32 [512], P('tm')
- grad_regress: float32 [1344, 1344], P('tm')
Inputs may be any that keep to these rules, and one draw needn't show every extreme that they name: `horizon`: every value is one of 96, 192, 336, 720, and each block of 3 consecutive series holds at least one with 720.
All inputs are finite; a program needn't handle non-finite values.
Results may differ from a plain program's by a relative error of at most 0.02.
Values may be sent and summed in bfloat16 or wider, within the bound.
No kernel may reach another device: no remote copies, remote signals or barrier semaphores. Data moves between devices by JAX's collectives and lax.ppermute only.
A program may use at most 384 MiB of HBM per device.

v0:
```python
import jax
import jax.numpy as jnp
from jax import lax
from jax.sharding import PartitionSpec as P

LEN = 1344


highest = lax.Precision.HIGHEST
epsilon = 1e-05


def passed_along(block, axis, distance):
    devices = range(lax.axis_size(axis))
    route = [(i - distance, i) for i in devices if i - distance in devices]
    return lax.ppermute(block, axis, route)


def layer_norm(field, gain_vec):
    centred = field - jnp.mean(field, axis=-1, keepdims=True)
    spread = jnp.mean(centred * centred, axis=-1, keepdims=True)
    return gain_vec * centred * lax.rsqrt(spread + epsilon)


def norm_back(field, gain_vec, upstream):
    unused, pullback = jax.vjp(layer_norm, field, gain_vec)
    return pullback(upstream)


def tanh_back(preact, upstream):
    unused, pullback = jax.vjp(jnp.tanh, preact)
    return pullback(upstream)[0]


def gelu_back(preact, upstream):
    unused, pullback = jax.vjp(jax.nn.gelu, preact)
    return pullback(upstream)[0]


def shear_table(out_rows, row_count, lag_count, first_row):
    table_shape = (out_rows, row_count, lag_count)
    target = lax.broadcasted_iota(jnp.int32, table_shape, 0)
    source = lax.broadcasted_iota(jnp.int32, table_shape, 1)
    offset = lax.broadcasted_iota(jnp.int32, table_shape, 2)
    return (target == first_row + source + offset).astype(jnp.float32)


def iso_forward(coarse, kernel):
    lag_count, features, slice_width = kernel.shape
    series = coarse.shape[0]

    def add_piece(running, shard_rows, first_row):
        row_count = shard_rows.shape[1]
        partial_value = jnp.einsum(
            "sjd,ldo->sjlo", shard_rows, kernel, preferred_element_type=jnp.float32
        )
        placing = shear_table(lag_count, row_count, lag_count, first_row)
        return jnp.einsum("ijl,sjlo->sio", placing, partial_value, precision=highest)

    initial = jnp.zeros((series, lag_count, slice_width), jnp.float32)
    return add_piece(initial, lax.all_gather(coarse, "tm", axis=1, tiled=True), jnp.int32(0))


def shear_all(grad_low):
    lag_count = grad_low.shape[1]
    placing = shear_table(lag_count, lag_count, lag_count, 0).astype(jnp.bfloat16)
    return jnp.einsum(
        "ijl,sio->sjlo", placing, grad_low, preferred_element_type=jnp.float32
    ).astype(jnp.bfloat16)


def iso_input_grad(sheared, kernel):
    return lax.psum_scatter(
        jnp.einsum("sjlo,ldo->jsd", sheared, kernel, preferred_element_type=jnp.float32).astype(
            jnp.bfloat16
        ),
        "tm",
        scatter_dimension=0,
        tiled=True,
    ).astype(jnp.float32)


def iso_kernel_grad(coarse, sheared, lag_count, slice_width):

    def add_piece(running, shard_rows, first_row):
        return jnp.einsum("sjd,sjlo->ldo", shard_rows, sheared, preferred_element_type=jnp.float32)

    initial = jnp.zeros((lag_count, coarse.shape[2], slice_width), jnp.float32)
    return add_piece(initial, lax.all_gather(coarse, "tm", axis=1, tiled=True), jnp.int32(0))


def shards(
    inputs,
    cotangent,
    horizon,
    down_a,
    down_b,
    up_a,
    up_b,
    iso_a,
    iso_b,
    merge,
    ffn_in,
    ffn_out,
    gain0,
    gain1,
    gain2,
    regress,
):
    series, length, features = inputs.shape
    rows_flat = series * length
    gathered = (
        lax.all_gather(down_a, "tm", axis=2, tiled=True),
        lax.all_gather(down_b, "tm", axis=2, tiled=True),
        lax.all_gather(up_a, "tm", axis=2, tiled=True),
        lax.all_gather(up_b, "tm", axis=2, tiled=True),
        lax.all_gather(merge, "tm", axis=2, tiled=True),
        lax.all_gather(ffn_in, "tm", axis=1, tiled=True),
        lax.all_gather(ffn_out, "tm", axis=1, tiled=True),
        lax.all_gather(gain0, "tm", axis=0, tiled=True),
        lax.all_gather(gain1, "tm", axis=0, tiled=True),
        lax.all_gather(gain2, "tm", axis=0, tiled=True),
    )
    gain_zero = gathered[7].astype(jnp.float32)
    gain_one = gathered[8].astype(jnp.float32)
    gain_two = gathered[9].astype(jnp.float32)
    margin = down_b.shape[0] // 2
    left_edge = passed_along(inputs[:, length - margin :, :], "tm", 1)
    inputs_wide = inputs.astype(jnp.float32)
    kernels = (iso_a, iso_b)
    records = []
    iso_cols = []
    for index in range(2):
        down_full = gathered[index]
        stride = down_full.shape[0]
        overhang = stride // 2
        row_total = length // stride
        extended = jnp.concatenate(
            [left_edge[:, margin - overhang :, :], inputs[:, : length - overhang, :]], axis=1
        )
        frames = extended.reshape(series * row_total, stride * features)
        down_pre = jnp.dot(
            frames,
            down_full.reshape(stride * features, features),
            preferred_element_type=jnp.float32,
        )
        down_pre = down_pre.reshape(series, row_total, features)
        coarse = jnp.tanh(down_pre).astype(jnp.bfloat16)
        iso_pre = iso_forward(coarse, kernels[index])
        records.append(
            {"frames": frames, "down_pre": down_pre, "coarse": coarse, "iso_pre": iso_pre}
        )
        iso_cols.append(jnp.tanh(iso_pre).astype(jnp.bfloat16))
    mixed_pair = (
        lax.all_to_all(iso_cols[0], "tm", split_axis=1, concat_axis=2, tiled=True),
        lax.all_to_all(iso_cols[1], "tm", split_axis=1, concat_axis=2, tiled=True),
    )
    for index in range(2):
        record = records[index]
        up_full = gathered[2 + index]
        upre_sum = mixed_pair[index].astype(jnp.float32) + record["coarse"].astype(jnp.float32)
        normed = layer_norm(upre_sum, gain_zero).astype(jnp.bfloat16)
        up_pre = jnp.einsum(
            "smd,kdo->smko", normed, up_full, preferred_element_type=jnp.float32
        ).reshape(series, length, features)
        scaled_sum = jnp.tanh(up_pre) + inputs_wide
        record["upre_sum"] = upre_sum
        record["normed"] = normed
        record["up_pre"] = up_pre
        record["scaled_sum"] = scaled_sum
        record["scaled"] = (
            layer_norm(scaled_sum, gain_zero).astype(jnp.bfloat16).reshape(rows_flat, features)
        )
    merge_full = gathered[4]
    merged = jnp.dot(records[0]["scaled"], merge_full[0], preferred_element_type=jnp.float32)
    merged = merged + jnp.dot(
        records[1]["scaled"], merge_full[1], preferred_element_type=jnp.float32
    )
    first = layer_norm(merged, gain_one).astype(jnp.bfloat16)
    hidden_pre = jnp.dot(first, gathered[5], preferred_element_type=jnp.float32)
    activated = jax.nn.gelu(hidden_pre).astype(jnp.bfloat16)
    back_proj = jnp.dot(activated, gathered[6], preferred_element_type=jnp.float32)
    season_sum = first.astype(jnp.float32) + back_proj
    season = layer_norm(season_sum, gain_two).astype(jnp.bfloat16).reshape(series, length, features)
    season_all = lax.all_gather(season, "tm", axis=1, tiled=True)
    trend = jnp.einsum("tu,sud->std", regress, season_all, preferred_element_type=jnp.float32)
    output = (season.astype(jnp.float32) + trend).astype(jnp.bfloat16)
    positions = lax.axis_index("tm") * length + jnp.arange(length, dtype=jnp.int32)
    valid_len = LEN - (720 - horizon) * LEN // 960
    loss_mask = (positions[None, :] < valid_len[:, None]).astype(jnp.float32)
    out_grad = (cotangent.astype(jnp.float32) * loss_mask[:, :, None]).astype(jnp.bfloat16)
    grad_regress = jnp.einsum(
        "std,sud->tu", out_grad, season_all, preferred_element_type=jnp.float32
    )
    back_rows = lax.psum_scatter(
        jnp.einsum("tu,std->usd", regress, out_grad, preferred_element_type=jnp.float32).astype(
            jnp.bfloat16
        ),
        "tm",
        scatter_dimension=0,
        tiled=True,
    ).astype(jnp.float32)
    season_grad = out_grad.astype(jnp.float32) + back_rows.transpose(1, 0, 2)
    sum_grad, grad_gain_two = norm_back(
        season_sum, gain_two, season_grad.reshape(rows_flat, features)
    )
    back_low = sum_grad.astype(jnp.bfloat16)
    grad_ffn_out = jnp.einsum("rf,rd->fd", activated, back_low, preferred_element_type=jnp.float32)
    act_grad = jnp.einsum("rd,fd->rf", back_low, gathered[6], preferred_element_type=jnp.float32)
    hidden_grad = gelu_back(hidden_pre, act_grad).astype(jnp.bfloat16)
    grad_ffn_in = jnp.einsum("rd,rf->df", first, hidden_grad, preferred_element_type=jnp.float32)
    first_grad = sum_grad + jnp.einsum(
        "rf,df->rd", hidden_grad, gathered[5], preferred_element_type=jnp.float32
    )
    merged_grad, grad_gain_one = norm_back(merged, gain_one, first_grad)
    merged_low = merged_grad.astype(jnp.bfloat16)
    input_grad = jnp.zeros((series, length, features), jnp.float32)
    left_grad = jnp.zeros((series, margin, features), jnp.float32)
    grad_gain_zero = jnp.zeros_like(gain_zero)
    merge_parts = []
    up_parts = []
    up_lows = []
    mixed_grads = []
    for index in range(2):
        record = records[index]
        up_full = gathered[2 + index]
        stride = up_full.shape[0]
        row_total = length // stride
        merge_parts.append(
            jnp.einsum(
                "rd,ro->do", record["scaled"], merged_low, preferred_element_type=jnp.float32
            )
        )
        scaled_grad = jnp.einsum(
            "ro,do->rd", merged_low, gathered[4][index], preferred_element_type=jnp.float32
        )
        sum_part, gain_part = norm_back(
            record["scaled_sum"], gain_zero, scaled_grad.reshape(series, length, features)
        )
        input_grad = input_grad + sum_part
        grad_gain_zero = grad_gain_zero + gain_part
        up_low = tanh_back(record["up_pre"], sum_part).astype(jnp.bfloat16)
        up_lows.append(up_low)
        up_rows = up_low.reshape(series * row_total, stride, features)
        normed_rows = record["normed"].reshape(series * row_total, features)
        up_parts.append(
            jnp.einsum("rd,rko->kdo", normed_rows, up_rows, preferred_element_type=jnp.float32)
        )
        normed_grad = jnp.einsum(
            "rko,kdo->rd", up_rows, up_full, preferred_element_type=jnp.float32
        )
        upre_grad, gain_part = norm_back(
            record["upre_sum"], gain_zero, normed_grad.reshape(series, row_total, features)
        )
        grad_gain_zero = grad_gain_zero + gain_part
        record["upre_grad"] = upre_grad
        mixed_grads.append(upre_grad.astype(jnp.bfloat16))
    mixed_back = (
        lax.all_to_all(mixed_grads[0], "tm", split_axis=2, concat_axis=1, tiled=True),
        lax.all_to_all(mixed_grads[1], "tm", split_axis=2, concat_axis=1, tiled=True),
    )
    down_parts = []
    down_lows = []
    kernel_grads = []
    for index in range(2):
        record = records[index]
        kernel = kernels[index]
        down_full = gathered[index]
        stride = down_full.shape[0]
        overhang = stride // 2
        row_total = length // stride
        iso_low = tanh_back(record["iso_pre"], mixed_back[index].astype(jnp.float32)).astype(
            jnp.bfloat16
        )
        sheared = shear_all(iso_low)
        coarse_iso = iso_input_grad(sheared, kernel)
        kernel_grads.append(
            iso_kernel_grad(record["coarse"], sheared, kernel.shape[0], kernel.shape[2])
        )
        coarse_grad = record["upre_grad"] + coarse_iso.transpose(1, 0, 2)
        down_low = tanh_back(record["down_pre"], coarse_grad).astype(jnp.bfloat16)
        down_lows.append(down_low)
        down_rows = down_low.reshape(series * row_total, features)
        down_grad = jnp.einsum(
            "rc,ro->co", record["frames"], down_rows, preferred_element_type=jnp.float32
        )
        down_parts.append(down_grad.reshape(stride, features, features))
        frame_grad = jnp.einsum(
            "ro,co->rc",
            down_rows,
            down_full.reshape(stride * features, features),
            preferred_element_type=jnp.float32,
        )
        frame_grad = frame_grad.reshape(series, length, features)
        input_grad = input_grad + jnp.pad(
            frame_grad[:, overhang:, :], ((0, 0), (0, overhang), (0, 0))
        )
        left_grad = left_grad + jnp.pad(
            frame_grad[:, :overhang, :], ((0, 0), (margin - overhang, 0), (0, 0))
        )
    right_back = passed_along(left_grad.astype(jnp.bfloat16), "tm", -1).astype(left_grad.dtype)
    input_grad = input_grad + jnp.pad(right_back, ((0, 0), (length - margin, 0), (0, 0)))
    grad_merge = jnp.stack(merge_parts)
    shares = (
        lax.psum_scatter(
            down_parts[0].astype(jnp.bfloat16), "tm", scatter_dimension=2, tiled=True
        ).astype(jnp.float32),
        lax.psum_scatter(
            down_parts[1].astype(jnp.bfloat16), "tm", scatter_dimension=2, tiled=True
        ).astype(jnp.float32),
        lax.psum_scatter(
            up_parts[0].astype(jnp.bfloat16), "tm", scatter_dimension=2, tiled=True
        ).astype(jnp.float32),
        lax.psum_scatter(
            up_parts[1].astype(jnp.bfloat16), "tm", scatter_dimension=2, tiled=True
        ).astype(jnp.float32),
        lax.psum_scatter(
            grad_merge.astype(jnp.bfloat16), "tm", scatter_dimension=2, tiled=True
        ).astype(jnp.float32),
        lax.psum_scatter(
            grad_ffn_in.astype(jnp.bfloat16), "tm", scatter_dimension=1, tiled=True
        ).astype(jnp.float32),
        lax.psum_scatter(
            grad_ffn_out.astype(jnp.bfloat16), "tm", scatter_dimension=1, tiled=True
        ).astype(jnp.float32),
        lax.psum_scatter(
            grad_gain_zero.astype(jnp.bfloat16), "tm", scatter_dimension=0, tiled=True
        ).astype(jnp.float32),
        lax.psum_scatter(
            grad_gain_one.astype(jnp.bfloat16), "tm", scatter_dimension=0, tiled=True
        ).astype(jnp.float32),
        lax.psum_scatter(
            grad_gain_two.astype(jnp.bfloat16), "tm", scatter_dimension=0, tiled=True
        ).astype(jnp.float32),
    )
    conv_pieces = (shares[0], shares[1], shares[2], shares[3])
    small_shares = (shares[4], shares[5], shares[6], shares[7], shares[8], shares[9])
    totals = lax.psum(
        (
            small_shares[0],
            small_shares[1],
            small_shares[2],
            small_shares[3],
            small_shares[4],
            small_shares[5],
            grad_regress,
        ),
        "series",
    )
    conv_totals = (
        lax.psum_scatter(conv_pieces[0], "series", scatter_dimension=1, tiled=True),
        lax.psum_scatter(conv_pieces[1], "series", scatter_dimension=1, tiled=True),
        lax.psum_scatter(conv_pieces[2], "series", scatter_dimension=1, tiled=True),
        lax.psum_scatter(conv_pieces[3], "series", scatter_dimension=1, tiled=True),
        lax.psum_scatter(kernel_grads[0], "series", scatter_dimension=1, tiled=True),
        lax.psum_scatter(kernel_grads[1], "series", scatter_dimension=1, tiled=True),
    )
    return (
        output,
        input_grad.astype(jnp.bfloat16),
        conv_totals[0],
        conv_totals[1],
        conv_totals[2],
        conv_totals[3],
        conv_totals[4],
        conv_totals[5],
        totals[0],
        totals[1],
        totals[2],
        totals[3],
        totals[4],
        totals[5],
        totals[6],
    )


def solution(mesh):
    return jax.shard_map(
        shards,
        mesh=mesh,
        in_specs=(
            P("series", "tm", None),
            P("series", "tm", None),
            P("series"),
            P(None, None, "tm"),
            P(None, None, "tm"),
            P(None, None, "tm"),
            P(None, None, "tm"),
            P(None, None, "tm"),
            P(None, None, "tm"),
            P(None, None, "tm"),
            P(None, "tm"),
            P(None, "tm"),
            P("tm"),
            P("tm"),
            P("tm"),
            P("tm", None),
        ),
        out_specs=(
            P("series", "tm", None),
            P("series", "tm", None),
            P(None, "series", "tm"),
            P(None, "series", "tm"),
            P(None, "series", "tm"),
            P(None, "series", "tm"),
            P(None, "series", "tm"),
            P(None, "series", "tm"),
            P(None, None, "tm"),
            P(None, "tm"),
            P(None, "tm"),
            P("tm"),
            P("tm"),
            P("tm"),
            P("tm", None),
        ),
        check_vma=False,
    )
```

profile of v0, /device:TPU:0, one launch (start us, length us, event | category | flops | bytes accessed | tf_op | source)
XLA Modules:
  0.0 2244.8 jit_solution(10028852016505325254)
XLA Ops:
  71.3 15.2 fusion.2
  86.5 19.3 fusion.85
  116.3 51.3 %all-gather.18.cloned.1.call-done = bf16[16,512,512]{2,1,0:T(8,128)(2,1)} async-done(((bf16[16,512,128]{2,1,0:T(8,128)(2,1)}), bf16[16,512,512]{2,1,0:T(8,128)(2,1)}) %all-gather.18.cloned.1.call-update) | async-done | bytes 8388624 | tf_op jit(solution)/shard_map/all_gather | solution.py:114
  198.3 18.9 all-gather.14.cloned.1.call-done
  230.6 47.6 %all-gather.20.cloned.1.call-done = bf16[16,512,512]{2,1,0:T(8,128)(2,1)} async-done(((bf16[16,512,128]{2,1,0:T(8,128)(2,1)}), bf16[16,512,512]{2,1,0:T(8,128)(2,1)}) %all-gather.20.cloned.1.call-update) | async-done | bytes 8388624 | tf_op jit(solution)/shard_map/all_gather | solution.py:116
  301.3 19.5 all-gather.22.cloned.1.call-done
  320.8 7.8 fusion.159
  328.6 16.7 all-gather.24.cloned.1.call-done
  359.1 9.9 fusion.20
  415.3 8.0 fusion.72
  429.3 11.9 fusion.65
  456.9 19.5 all-reduce.18.cloned.1.call-done
  482.2 15.0 copy.171
  497.2 13.8 copy.179
  520.5 15.3 copy.173
  535.8 18.2 copy.181
  563.1 8.8 convolution_convert_fusion.3
  588.8 23.1 %reduce-scatter.35.cloned.1.call-done = bf16[16,512,128]{1,2,0:T(8,128)(2,1)} async-done(((bf16[16,512,512]{1,2,0:T(8,128)(2,1)}), bf16[16,512,128]{1,2,0:T(8,128)(2,1)}) %reduce-scatter.35.cloned.1.call-update) | async-done | bytes 2097168 | tf_op jit(solution)/shard_map/reduce_scatter | solution.py:314
  617.6 14.1 convolution_bitcast_fusion.1
  631.6 24.2 %copy.144 = f32[84,512,128]{2,0,1:T(8,128)} copy(f32[84,512,128]{1,2,0:T(8,128)} %convolution_bitcast_fusion.1) | data formatting | bytes 44040192 | tf_op jit(solution)/shard_map/sjd,sjlo->ldo/transpose | solution.py:86
  657.0 20.5 convolution_bitcast_fusion
  677.5 27.9 %copy.141 = f32[112,512,128]{2,0,1:T(8,128)} copy(f32[112,512,128]{1,2,0:T(8,128)} %convolution_bitcast_fusion) | data formatting | bytes 58720256 | tf_op jit(solution)/shard_map/sjd,sjlo->ldo/transpose | solution.py:86
  721.7 61.0 %reduce-scatter.47.cloned.1.call-done = bf16[128,8192]{1,0:T(8,128)(2,1)} async-done(((bf16[512,8192]{1,0:T(8,128)(2,1)}), bf16[128,8192]{1,0:T(8,128)(2,1)}) %reduce-scatter.47.cloned.1.call-update) | async-done | bytes 2097168
  823.3 21.3 reduce-scatter.51.cloned.1.call-done
  845.9 33.3 %reduce-scatter.43.cloned.1.call-done = bf16[512,512]{1,0:T(8,128)(2,1)} async-done(((bf16[512,2048]{1,0:T(8,128)(2,1)}), bf16[512,512]{1,0:T(8,128)(2,1)}) %reduce-scatter.43.cloned.1.call-update) | async-done | bytes 524304 | tf_op jit(solution)/shard_map/reduce_scatter | solution.py:320
  879.2 137.8 %all-reduce.19 = (f32[2,512,128]{2,1,0:T(8,128)}, f32[512,512]{1,0:T(8,128)}, f32[2048,128]{1,0:T(8,128)}, f32[128]{0:T(128)}, f32[128]{0:T(128)}, /*index=5*/f32[128]{0:T(128)}) all-reduce(bf16[2,512,128]{2,1,0:T(8,128)(2,1)S(1)} %copy.176, ...), channel_id=1, replica_groups=mesh['series'=8,'tm'=4] {'series'}, use_global_device_ids=true, to_apply=%region_38.39 | all-reduce | flops 655744 | bytes 3935232 | tf_op jit(solution)/shard_map/psum | solution.py:338
  1030.0 88.2 %reduce-scatter.37.cloned.1.call-done = f32[16,64,128]{2,0,1:T(8,128)} async-done(((f32[16,512,128]{2,0,1:T(8,128)}), f32[16,64,128]{2,0,1:T(8,128)}) %reduce-scatter.37.cloned.1.call-update) | async-done | bytes 524304 | tf_op jit(solution)/shard_map/reduce_scatter | solution.py:354
  1120.2 375.2 %reduce-scatter.41.cloned.1.call-done = f32[84,64,128]{2,0,1:T(8,128)} async-done(((f32[84,512,128]{2,0,1:T(8,128)}), f32[84,64,128]{2,0,1:T(8,128)}) %reduce-scatter.41.cloned.1.call-update) | async-done | bytes 2752528 | tf_op jit(solution)/shard_map/reduce_scatter | solution.py:356
  1499.3 463.3 %reduce-scatter.39.cloned.1.call-done = f32[112,64,128]{2,0,1:T(8,128)} async-done(((f32[112,512,128]{2,0,1:T(8,128)}), f32[112,64,128]{2,0,1:T(8,128)}) %reduce-scatter.39.cloned.1.call-update) | async-done | bytes 3670032 | tf_op jit(solution)/shard_map/reduce_scatter | solution.py:355
  1967.6 95.2 %all-reduce.16.cloned.1.call-done = f32[336,1344]{1,0:T(8,128)} async-done(((f32[336,1344]{1,0:T(8,128)}), f32[336,1344]{1,0:T(8,128)}) %all-reduce.16.cloned.1.call-update) | async-done | bytes 1806352 | tf_op jit(solution)/shard_map/psum | solution.py:338
  2062.9 79.5 %reduce-scatter.27.cloned.1.call-done = f32[12,64,128]{2,1,0:T(8,128)} async-done(((f32[12,512,128]{2,1,0:T(8,128)}), f32[12,64,128]{2,1,0:T(8,128)}) %reduce-scatter.27.cloned.1.call-update) | async-done | bytes 393232 | tf_op jit(solution)/shard_map/reduce_scatter | solution.py:351
  2142.4 92.3 %reduce-scatter.29.cloned.1.call-done = f32[16,64,128]{2,1,0:T(8,128)} async-done(((f32[16,512,128]{2,1,0:T(8,128)}), f32[16,64,128]{2,1,0:T(8,128)}) %reduce-scatter.29.cloned.1.call-update) | async-done | bytes 524304 | tf_op jit(solution)/shard_map/reduce_scatter | solution.py:352
  (426 shorter events, 352.9 us)
Async XLA Ops:
  7.2 52.4 %all-gather.12.cloned.1.call-start = ((), (), s32[]{:S(2)}) async-start(), calls=%async_computation.18 | async-start | bytes 7864320 | tf_op jit(solution)/shard_map/all_gather | solution.py:113
  7.9 102.6 %reduce-scatter.25.cloned.1.call-start = ((), (), s32[]{:S(2)}) async-start(), calls=%async_computation.26 | async-start | bytes 5160960 | tf_op jit(solution)/shard_map/reduce_scatter | solution.py:195
  14.5 153.1 %all-gather.18.cloned.1.call-start = ((), (), s32[]{:S(2)}) async-start(), calls=%async_computation.21 | async-start | bytes 10485760 | tf_op jit(solution)/shard_map/all_gather | solution.py:114
  15.2 202.0 %all-gather.14.cloned.1.call-start = ((), (), s32[]{:S(2)}) async-start(), calls=%async_computation.19 | async-start | bytes 7864320 | tf_op jit(solution)/shard_map/all_gather | solution.py:115
  15.8 262.3 %all-gather.20.cloned.1.call-start = ((), (), s32[]{:S(2)}) async-start(), calls=%async_computation.22 | async-start | bytes 10485760 | tf_op jit(solution)/shard_map/all_gather | solution.py:116
  16.4 280.1 %all-gather.16.cloned.1.call-start = ((), (), s32[]{:S(2)}) async-start(), calls=%async_computation.20 | async-start | bytes 1310720 | tf_op jit(solution)/shard_map/all_gather | solution.py:117
  17.0 303.8 %all-gather.22.cloned.1.call-start = ((), (), s32[]{:S(2)}) async-start(), calls=%async_computation.23 | async-start | bytes 2621440 | tf_op jit(solution)/shard_map/all_gather | solution.py:118
  17.7 327.5 %all-gather.24.cloned.1.call-start = ((), (), s32[]{:S(2)}) async-start(), calls=%async_computation.24 | async-start | bytes 2621440 | tf_op jit(solution)/shard_map/all_gather | solution.py:119
  17.8 31.3 %collective-permute-start = (bf16[3,8,512]{2,1,0:T(8,128)(2,1)S(1)}, bf16[3,8,512]{2,1,0:T(8,128)(2,1)S(1)}, u32[]{:S(2)}, u32[]{:S(2)}) collective-permute-start(bf16[3,8,512]{2,1,0:T(8,128)(2,1)S(1)} %slice.32), channel_id=1, source_target_pairs={{0,1},{1,2},{2,3},{4,5},{5,6},{6,7},{8,9},{9,10},{10,11},{12,13},{... | collective-permute-start | bytes 73736 | tf_op jit(solution)/shard_map/ppermute | solution.py:16
  34.5 337.9 %copy-start.60 = (f32[4,1,128]{2,1,0:T(1,128)}, f32[4,1,128]{2,1,0:T(1,128)S(1)}, u32[]{:S(2)}) copy-start(f32[4,1,128]{2,1,0:T(1,128)S(1)} %convert_element_type.392) | copy-start | bytes 6148
  107.2 7.7 all-to-all-start
  194.0 35.1 %all-to-all-start.1 = ((bf16[3,84,128]{2,0,1:T(4,128)(2,1)}), bf16[3,84,128]{2,0,1:T(4,128)(2,1)}, u32[]{:S(2)}, u32[]{:S(2)}) async-start(bf16[3,84,128]{2,0,1:T(4,128)(2,1)} %copy.121), calls=%async_computation.1 | async-start | bytes 172032 | tf_op jit(solution)/shard_map/all_to_all | solution.py:156
  388.3 17.3 all-to-all-start.3
  405.6 17.7 all-to-all-start.2
  408.9 67.5 %all-reduce.18.cloned.1.call-start = ((), (), s32[]{:S(2)}) async-start(), calls=%async_computation.41 | async-start | bytes 1228800
  441.3 142.7 %reduce-scatter.31.cloned.1.call-start = ((), (), s32[]{:S(2)}) async-start(), calls=%async_computation.29 | async-start | bytes 7864320 | tf_op jit(solution)/shard_map/reduce_scatter | solution.py:311
  446.2 165.7 %reduce-scatter.35.cloned.1.call-start = ((), (), s32[]{:S(2)}) async-start(), calls=%async_computation.31 | async-start | bytes 10485760 | tf_op jit(solution)/shard_map/reduce_scatter | solution.py:314
  453.1 252.4 %all-gather.26.cloned.1.call-start = ((), (), s32[]{:S(2)}) async-start(), calls=%async_computation.25 | async-start | bytes 5160960 | tf_op jit(solution)/shard_map/all_gather | solution.py:185
  453.7 258.3 %reduce-scatter.45.cloned.1.call-start = ((), (), s32[]{:S(2)}) async-start(), calls=%async_computation.37 | async-start | bytes 7864320
  511.0 271.7 %reduce-scatter.47.cloned.1.call-start = ((), (), s32[]{:S(2)}) async-start(), calls=%async_computation.38 | async-start | bytes 10485760
  554.0 267.7 %reduce-scatter.49.cloned.1.call-start = ((), (), s32[]{:S(2)}) async-start(), calls=%async_computation.39 | async-start | bytes 1310720
  563.1 281.5 %reduce-scatter.51.cloned.1.call-start = ((), (), s32[]{:S(2)}) async-start(), calls=%async_computation.40 | async-start | bytes 2621440
  576.0 303.2 %reduce-scatter.43.cloned.1.call-start = ((), (), s32[]{:S(2)}) async-start(), calls=%async_computation.35 | async-start | bytes 2621440 | tf_op jit(solution)/shard_map/reduce_scatter | solution.py:320
  583.9 444.2 %reduce-scatter.33.cloned.1.call-start = ((), (), s32[]{:S(2)}) async-start(), calls=%async_computation.30 | async-start | bytes 4718592 | tf_op jit(solution)/shard_map/reduce_scatter | solution.py:353
  588.7 529.5 %reduce-scatter.37.cloned.1.call-start = ((), (), s32[]{:S(2)}) async-start(), calls=%async_computation.32 | async-start | bytes 4718592 | tf_op jit(solution)/shard_map/reduce_scatter | solution.py:354
  616.6 878.8 %reduce-scatter.41.cloned.1.call-start = ((), (), s32[]{:S(2)}) async-start(), calls=%async_computation.34 | async-start | bytes 25952256 | tf_op jit(solution)/shard_map/reduce_scatter | solution.py:356
  655.9 1306.7 %reduce-scatter.39.cloned.1.call-start = ((), (), s32[]{:S(2)}) async-start(), calls=%async_computation.33 | async-start | bytes 33030144 | tf_op jit(solution)/shard_map/reduce_scatter | solution.py:355
  705.4 1357.4 %all-reduce.16.cloned.1.call-start = ((), (), s32[]{:S(2)}) async-start(), calls=%async_computation.36 | async-start | bytes 3784704 | tf_op jit(solution)/shard_map/psum | solution.py:338
  712.0 1430.4 %reduce-scatter.27.cloned.1.call-start = ((), (), s32[]{:S(2)}) async-start(), calls=%async_computation.27 | async-start | bytes 3538944 | tf_op jit(solution)/shard_map/reduce_scatter | solution.py:351
  721.6 1513.0 %reduce-scatter.29.cloned.1.call-start = ((), (), s32[]{:S(2)}) async-start(), calls=%async_computation.28 | async-start | bytes 4718592 | tf_op jit(solution)/shard_map/reduce_scatter | solution.py:352
  815.8 3.1 collective-permute-start.1
  821.8 195.3 %copy-start.35 = (bf16[1008,512]{1,0:T(8,128)(2,1)S(1)}, bf16[1008,512]{1,0:T(8,128)(2,1)}, u32[]{:S(2)}) copy-start(bf16[1008,512]{1,0:T(8,128)(2,1)} %get-tuple-element.117) | copy-start | bytes 3096580
  (91 other events, 877.4 us)
Sparse Core Ops, SparseCore 0:
  9.6 49.9 all-gather.11
  62.1 44.3 reduce-scatter.24
  108.1 59.3 all-gather.17
  169.1 48.1 all-gather.13
  218.7 59.3 all-gather.19
  279.6 16.8 all-gather.15
  298.1 22.5 all-gather.21
  322.4 22.8 all-gather.23
  441.4 34.9 all-reduce.17
  479.0 58.5 reduce-scatter.30
  540.1 71.6 reduce-scatter.34
  613.3 34.1 all-gather.25
  650.2 58.3 reduce-scatter.44
  711.0 71.7 reduce-scatter.46
  785.8 24.8 reduce-scatter.48
  813.1 31.4 reduce-scatter.50
  847.7 31.4 reduce-scatter.42
  882.7 145.3 reduce-scatter.32
  1032.2 86.0 reduce-scatter.36
  1121.9 373.3 reduce-scatter.40
  1499.3 463.2 reduce-scatter.38
  1966.8 96.0 all-reduce.15
  2067.5 74.8 reduce-scatter.26
  2146.8 87.7 reduce-scatter.28
where the time goes:
time: 2260 us; the launch traced here: 2240 us
  waiting for transfers between devices  1530 us (68%)
  matrix products  235 us (10%)
  local copies, waits for them, and re-layouts  228 us (10%)
  blocking collectives  174 us (8%)
  other arithmetic  38.9 us (2%)
    reduce_scatter x1, waiting for transfers between devices, shards(): lax.psum_scatter(kernel_grads[0], 'series', scatter_dimension=1, tiled=True)  463 us
    reduce_scatter x1, waiting for transfers between devices, shards(): lax.psum_scatter(kernel_grads[1], 'series', scatter_dimension=1, tiled=True)  375 us
    psum x1, blocking collectives, shards(): lax.psum((small_shares[0], small_shares[1], small_shares[2], small_shares...  138 us
    unnamed x207, local copies, waits for them, and re-layouts  130 us
    unnamed x29, waiting for transfers between devices  106 us
    psum x1, waiting for transfers between devices, shards(): lax.psum((small_shares[0], small_shares[1], small_shares[2], small_shares...  95.2 us
    reduce_scatter x1, waiting for transfers between devices, shards(): lax.psum_scatter(conv_pieces[1], 'series', scatter_dimension=1, tiled=True)  92.3 us
    reduce_scatter x1, waiting for transfers between devices, shards(): lax.psum_scatter(conv_pieces[3], 'series', scatter_dimension=1, tiled=True)  88.2 us
  transfers between devices with their start and end apart: 30, of which 21 were waited for; matrix products, arithmetic and copies ran while one was open for 19% of the time, Pallas kernels for 0%

commit v1 on v0

v1 whole, which is shorter than its diff:
```python
import functools

import jax
import jax.numpy as jnp
from jax import lax
from jax.experimental import pallas as pl
from jax.experimental.pallas import tpu as pltpu
from jax.sharding import PartitionSpec as P

LEN = 1344
SHIFTS = 16

epsilon = 1e-05
bf16 = jnp.bfloat16
f32 = jnp.float32


def dot32(spec, a, b):
    return jnp.einsum(spec, a, b, preferred_element_type=f32)


def norm_parts(field):
    centred = field - jnp.mean(field, axis=-1, keepdims=True)
    spread = jnp.mean(centred * centred, axis=-1, keepdims=True)
    scale = lax.rsqrt(spread + epsilon)
    return centred * scale, scale


def layer_norm(field, gain_vec):
    return gain_vec * norm_parts(field)[0]


def norm_back(field, gain_vec, upstream):
    unit, scale = norm_parts(field)
    lifted = gain_vec * upstream
    mean_lift = jnp.mean(lifted, axis=-1, keepdims=True)
    mean_both = jnp.mean(lifted * unit, axis=-1, keepdims=True)
    gain_grad = jnp.sum(upstream * unit, axis=tuple(range(upstream.ndim - 1)))
    return (lifted - mean_lift - unit * mean_both) * scale, gain_grad


def gelu_back(preact, upstream):
    unused, pullback = jax.vjp(jax.nn.gelu, preact)
    return pullback(upstream)[0]


def padded_rows(count):
    return -(-count // 16) * 16


def lag_block(count):
    return max(n for n in range(2, 15, 2) if count % n == 0)


def iso_forward_body(series, rows, lags, coarse_ref, kernel_ref, out_ref, total_ref):
    step = pl.program_id(0)

    @pl.when(step == 0)
    def clear():
        total_ref[...] = jnp.zeros_like(total_ref)

    coarse = coarse_ref[...]
    for pair in range(lags // 2):
        both = jnp.concatenate([kernel_ref[2 * pair], kernel_ref[2 * pair + 1]], axis=1)
        part = jnp.dot(coarse, both, preferred_element_type=f32)
        width = part.shape[1] // 2
        for half in range(2):
            place = pl.ds(step * lags + 2 * pair + half, rows)
            for s in range(series):
                total_ref[s, place, :] += part[
                    s * rows : (s + 1) * rows, half * width : (half + 1) * width
                ]

    @pl.when(step == pl.num_programs(0) - 1)
    def finish():
        out_ref[...] = total_ref[:, :rows, :]


def iso_forward(coarse, kernel):
    lag_count, features, width = kernel.shape
    series = coarse.shape[0]
    rows = padded_rows(lag_count)
    lags = lag_block(lag_count)
    coarse = jnp.pad(coarse, ((0, 0), (0, rows - lag_count), (0, 0)))
    out = pl.pallas_call(
        functools.partial(iso_forward_body, series, rows, lags),
        grid=(lag_count // lags,),
        in_specs=[
            pl.BlockSpec((series * rows, features), lambda i: (0, 0)),
            pl.BlockSpec((lags, features, width), lambda i: (i, 0, 0)),
        ],
        out_specs=pl.BlockSpec((series, rows, width), lambda i: (0, 0, 0)),
        out_shape=jax.ShapeDtypeStruct((series, rows, width), f32),
        scratch_shapes=[pltpu.VMEM((series, 2 * rows, width), f32)],
        compiler_params=pltpu.CompilerParams(vmem_limit_bytes=40 * 2**20),
        cost_estimate=pl.CostEstimate(
            flops=2 * series * rows * lag_count * features * width,
            bytes_accessed=2 * lag_count * features * width,
            transcendentals=0,
        ),
    )(coarse.reshape(series * rows, features), kernel)
    return out[:, :lag_count, :]


def iso_back_body(series, rows, lags, grad_ref, kernel_ref, out_ref):
    step = pl.program_id(0)

    @pl.when(step == 0)
    def clear():
        out_ref[...] = jnp.zeros_like(out_ref)

    kernel = jnp.concatenate([kernel_ref[n] for n in range(lags)], axis=1)
    pieces = []
    for s in range(series):
        shifted = [
            grad_ref[s, pl.ds(step * lags + n, rows), :].astype(bf16) for n in range(lags)
        ]
        pieces.append(jnp.concatenate(shifted, axis=1))
    sheared = jnp.concatenate(pieces, axis=0)
    out_ref[...] += lax.dot_general(
        sheared, kernel, (((1,), (1,)), ((), ())), preferred_element_type=f32
    )


def iso_back(grad, kernel):
    lag_count, features, width = kernel.shape
    series = grad.shape[0]
    rows = padded_rows(lag_count)
    lags = lag_block(lag_count)
    grad = jnp.pad(grad.astype(f32), ((0, 0), (0, 2 * rows - lag_count), (0, 0)))
    out = pl.pallas_call(
        functools.partial(iso_back_body, series, rows, lags),
        grid=(lag_count // lags,),
        in_specs=[
            pl.BlockSpec((series, 2 * rows, width), lambda i: (0, 0, 0)),
            pl.BlockSpec((lags, features, width), lambda i: (i, 0, 0)),
        ],
        out_specs=pl.BlockSpec((series * rows, features), lambda i: (0, 0)),
        out_shape=jax.ShapeDtypeStruct((series * rows, features), f32),
        compiler_params=pltpu.CompilerParams(vmem_limit_bytes=40 * 2**20),
        cost_estimate=pl.CostEstimate(
            flops=2 * series * rows * lag_count * features * width,
            bytes_accessed=2 * lag_count * features * width,
            transcendentals=0,
        ),
    )(grad, kernel)
    return out.reshape(series, rows, features)[:, :lag_count, :]


def iso_kernel_grad(coarse_all, grad_all):
    series, lag_count, part = coarse_all.shape
    width = grad_all.shape[2]
    blocks = -(-lag_count // SHIFTS)
    source = coarse_all.transpose(1, 0, 2)
    source = jnp.pad(source, ((SHIFTS, 0), (0, 0), (0, 0)))
    stacked = jnp.stack(
        [source[SHIFTS - p : SHIFTS - p + lag_count] for p in range(SHIFTS)], axis=2
    )
    stacked = stacked.reshape(lag_count * series, SHIFTS * part)
    target = grad_all.transpose(1, 0, 2)
    target = jnp.pad(target, ((0, blocks * SHIFTS), (0, 0), (0, 0)))
    moved = jnp.stack(
        [target[q * SHIFTS : q * SHIFTS + lag_count] for q in range(blocks)], axis=2
    )
    moved = moved.reshape(lag_count * series, blocks * width)
    total = dot32("ra,rb->ab", stacked, moved).reshape(SHIFTS, part, blocks, width)
    return total.transpose(2, 0, 1, 3).reshape(blocks * SHIFTS, part, width)[:lag_count]


def to_time(block):
    series, length, width = block.shape
    count = lax.axis_size("tm")
    parts = block.reshape(series, count, length // count, width).transpose(1, 0, 2, 3)
    moved = lax.all_to_all(parts, "tm", split_axis=0, concat_axis=0, tiled=True)
    return moved.transpose(1, 2, 0, 3).reshape(series, length // count, count * width)


def to_channels(block):
    series, length, features = block.shape
    count = lax.axis_size("tm")
    parts = block.reshape(series, length, count, features // count).transpose(2, 0, 1, 3)
    moved = lax.all_to_all(parts, "tm", split_axis=0, concat_axis=0, tiled=True)
    return moved.transpose(1, 0, 2, 3).reshape(series, count * length, features // count)


def gather_channels(block):
    rows, width = block.shape
    count = lax.axis_size("tm")
    whole = lax.all_gather(block, "tm", axis=0, tiled=False)
    return whole.transpose(1, 0, 2).reshape(rows, count * width)


def scatter_channels(partial, extra=None):
    rows, features = partial.shape
    count = lax.axis_size("tm")
    width = features // count
    parts = partial.astype(bf16).reshape(rows, count, width).transpose(1, 0, 2)
    tail = 0
    if extra is not None:
        flat = extra.reshape(-1)
        tail = -(-flat.shape[0] // width)
        flat = jnp.pad(flat, (0, tail * width - flat.shape[0])).reshape(tail, width)
        high = flat.astype(bf16)
        low = (flat - high.astype(f32)).astype(bf16)
        more = jnp.broadcast_to(
            jnp.concatenate([high, low])[None], (count, 2 * tail, width)
        )
        parts = jnp.concatenate([parts, more], axis=1)
    moved = lax.all_to_all(parts, "tm", split_axis=0, concat_axis=0, tiled=True)
    total = jnp.sum(moved.astype(f32), axis=0)
    if extra is None:
        return total
    sums = total[rows : rows + tail] + total[rows + tail :]
    return total[:rows], sums.reshape(-1)[: extra.size].reshape(extra.shape)


def shards(
    inputs,
    cotangent,
    horizon,
    down_a,
    down_b,
    up_a,
    up_b,
    iso_a,
    iso_b,
    merge,
    ffn_in,
    ffn_out,
    gain0,
    gain1,
    gain2,
    regress,
):
    series, length, features = inputs.shape
    rows_flat = series * length
    tm = lax.axis_index("tm")
    count = lax.axis_size("tm")
    width = features // count
    whole_length = length * count
    downs, ups, isos = (down_a, down_b), (up_a, up_b), (iso_a, iso_b)
    strides = (down_a.shape[0], down_b.shape[0])
    coarse_rows = [whole_length // k for k in strides]
    both_rows = sum(coarse_rows)

    inputs_all = lax.all_gather(inputs, "tm", axis=1, tiled=True)
    gains = lax.all_gather(jnp.stack([gain0, gain1, gain2]), "tm", axis=1, tiled=True)
    gain_zero, gain_one, gain_two = [gains[n].astype(f32) for n in range(3)]
    merge_full = lax.all_gather(merge, "tm", axis=2, tiled=True)
    ffn_in_full = lax.all_gather(ffn_in, "tm", axis=1, tiled=True)
    ffn_out_full = lax.all_gather(ffn_out, "tm", axis=1, tiled=True)
    inputs_wide = inputs.astype(f32)
    inputs_part = lax.all_to_all(
        inputs_all, "series", split_axis=2, concat_axis=0, tiled=True
    )

    positions = tm * length + jnp.arange(length, dtype=jnp.int32)
    valid_len = LEN - (720 - horizon) * LEN // 960
    loss_mask = (positions[None, :] < valid_len[:, None]).astype(f32)
    out_grad = (cotangent.astype(f32) * loss_mask[:, :, None]).astype(bf16)
    back_rows = lax.psum_scatter(
        dot32("tu,std->usd", regress, out_grad).astype(bf16),
        "tm",
        scatter_dimension=0,
        tiled=True,
    ).astype(f32)

    def split_rows(both):
        shaped = both.reshape(series, both_rows, both.shape[-1])
        return shaped[:, : coarse_rows[0]], shaped[:, coarse_rows[0] :]

    def join_rows(pair):
        joined = jnp.concatenate(pair, axis=1)
        return joined.reshape(series * both_rows, joined.shape[-1])

    down_pre = []
    for down, stride in zip(downs, strides):
        overhang = stride // 2
        down_pre.append(
            lax.conv_general_dilated(
                inputs_all,
                down,
                window_strides=(stride,),
                padding=[(overhang, -overhang)],
                dimension_numbers=("NWC", "WIO", "NWC"),
                preferred_element_type=f32,
            )
        )
    coarse_tanh = jnp.tanh(join_rows(down_pre))
    coarse_own = coarse_tanh.astype(bf16)
    coarse_both = gather_channels(coarse_own)
    coarse_pair = split_rows(coarse_both)
    coarse_part = lax.all_to_all(
        coarse_both.reshape(series, both_rows, features),
        "series",
        split_axis=2,
        concat_axis=0,
        tiled=True,
    )
    iso_tanh = jnp.tanh(
        join_rows([iso_forward(coarse_pair[n], isos[n]) for n in range(2)])
    )
    mixed_both = gather_channels(iso_tanh.astype(bf16))
    upre_sum = mixed_both.astype(f32) + coarse_both.astype(f32)
    upre_unit, upre_scale = norm_parts(upre_sum)
    normed_pair = split_rows((gain_zero * upre_unit).astype(bf16))

    up_tanh = []
    scaled_sum = []
    scaled = []
    for n in range(2):
        up_pre = dot32("smd,kdo->smko", normed_pair[n], ups[n])
        up_tanh.append(jnp.tanh(up_pre.reshape(series, whole_length, width)))
        scaled_sum.append(to_time(up_tanh[n].astype(bf16)).astype(f32) + inputs_wide)
        scaled.append(
            layer_norm(scaled_sum[n], gain_zero).astype(bf16).reshape(rows_flat, features)
        )
    merged = dot32("rd,do->ro", scaled[0], merge_full[0])
    merged = merged + dot32("rd,do->ro", scaled[1], merge_full[1])
    first = layer_norm(merged, gain_one).astype(bf16)
    hidden_pre = dot32("rd,df->rf", first, ffn_in_full)
    activated = jax.nn.gelu(hidden_pre).astype(bf16)
    back_proj = dot32("rf,fd->rd", activated, ffn_out_full)
    season_sum = first.astype(f32) + back_proj
    season = layer_norm(season_sum, gain_two).astype(bf16).reshape(series, length, features)
    season_all = lax.all_gather(season, "tm", axis=1, tiled=True)
    trend = dot32("tu,sud->std", regress, season_all)
    output = (season.astype(f32) + trend).astype(bf16)
    grad_regress = lax.psum(
        dot32("std,sud->tu", out_grad, season_all).astype(bf16), "series"
    ).astype(f32)

    season_grad = out_grad.astype(f32) + back_rows.transpose(1, 0, 2)
    sum_grad, grad_gain_two = norm_back(
        season_sum, gain_two, season_grad.reshape(rows_flat, features)
    )
    back_low = sum_grad.astype(bf16)
    grad_ffn_out = dot32("rf,rd->fd", activated, back_low).astype(bf16)
    act_grad = dot32("rd,fd->rf", back_low, ffn_out_full)
    hidden_grad = gelu_back(hidden_pre, act_grad).astype(bf16)
    grad_ffn_in = dot32("rd,rf->df", first, hidden_grad).astype(bf16)
    first_grad = sum_grad + dot32("rf,df->rd", hidden_grad, ffn_in_full)
    merged_grad, grad_gain_one = norm_back(merged, gain_one, first_grad)
    merged_low = merged_grad.astype(bf16)
    grad_merge = jnp.stack(
        [dot32("rd,ro->do", scaled[n], merged_low) for n in range(2)]
    ).astype(bf16)
    weight_grads = tuple(
        lax.psum_scatter(grad, "tm", scatter_dimension=grad.ndim - 1, tiled=True)
        for grad in (grad_merge, grad_ffn_in, grad_ffn_out)
    )
    weight_grads = lax.psum(weight_grads, "series")

    input_grad = jnp.zeros((series, length, features), f32)
    grad_gain_zero = jnp.zeros_like(gain_zero)
    grad_ups = []
    normed_grads = []
    for n in range(2):
        scaled_grad = dot32("ro,do->rd", merged_low, merge_full[n])
        sum_part, gain_part = norm_back(
            scaled_sum[n], gain_zero, scaled_grad.reshape(series, length, features)
        )
        input_grad = input_grad + sum_part
        grad_gain_zero = grad_gain_zero + gain_part
        arrived = to_channels(sum_part.astype(bf16)).astype(f32)
        up_low = (arrived * (1.0 - up_tanh[n] * up_tanh[n])).astype(bf16)
        up_rows = up_low.reshape(series, coarse_rows[n], strides[n], width)
        grad_ups.append(
            lax.psum_scatter(
                dot32("smd,smko->kdo", normed_pair[n], up_rows).astype(bf16),
                "series",
                scatter_dimension=1,
                tiled=True,
            ).astype(f32)
        )
        normed_grads.append(dot32("smko,kdo->smd", up_rows, ups[n]))
    normed_partial = join_rows(normed_grads)
    lifted_partial = gain_zero * normed_partial
    lifted_sums = jnp.stack(
        [jnp.sum(lifted_partial, axis=-1), jnp.sum(lifted_partial * upre_unit, axis=-1)]
    )
    normed_grad, lifted_sums = scatter_channels(normed_partial, lifted_sums)
    unit_own = lax.dynamic_slice_in_dim(upre_unit, tm * width, width, axis=1)
    gain_own = lax.dynamic_slice_in_dim(gain_zero, tm * width, width, axis=0)
    lifted_means = lifted_sums[:, :, None] / features
    upre_grad = (
        gain_own * normed_grad - lifted_means[0] - unit_own * lifted_means[1]
    ) * upre_scale
    gain_own_part = jnp.sum(normed_grad * unit_own, axis=0)
    iso_low = (
        upre_grad.astype(bf16).astype(f32) * (1.0 - iso_tanh * iso_tanh)
    ).astype(bf16)
    iso_low_all = lax.all_gather(
        iso_low.reshape(series, both_rows, width), "series", axis=0, tiled=True
    )
    iso_low_pair = split_rows(iso_low)
    coarse_iso = scatter_channels(
        join_rows([iso_back(iso_low_pair[n], isos[n]) for n in range(2)])
    )
    coarse_grad = upre_grad + coarse_iso
    down_low = (coarse_grad * (1.0 - coarse_tanh * coarse_tanh)).astype(bf16)
    down_low_all = lax.all_gather(
        down_low.reshape(series, both_rows, width), "series", axis=0, tiled=True
    )
    down_low_pair = split_rows(down_low)
    frames_partial = jnp.zeros((series, whole_length, features), f32)
    for n in range(2):
        overhang = strides[n] // 2
        frame_grad = dot32("smo,kco->smkc", down_low_pair[n], downs[n])
        frame_grad = frame_grad.reshape(series, whole_length, features)
        frames_partial = frames_partial + jnp.pad(
            frame_grad[:, overhang:], ((0, 0), (0, overhang), (0, 0))
        )
    frames_total = lax.psum_scatter(
        frames_partial.astype(bf16), "tm", scatter_dimension=1, tiled=True
    )
    input_grad = (input_grad + frames_total.astype(f32)).astype(bf16)

    first_rows = (0, coarse_rows[0])
    grad_downs = []
    grad_isos = []
    all_series = inputs_part.shape[0]
    for n in range(2):
        rows = slice(first_rows[n], first_rows[n] + coarse_rows[n])
        overhang = strides[n] // 2
        frames = jnp.pad(inputs_part, ((0, 0), (overhang, 0), (0, 0)))[:, :whole_length]
        frames = frames.reshape(all_series, coarse_rows[n], strides[n], -1)
        grad_downs.append(dot32("smkc,smo->kco", frames, down_low_all[:, rows]))
        grad_isos.append(iso_kernel_grad(coarse_part[:, rows], iso_low_all[:, rows]))

    own_gain = lax.dynamic_update_slice_in_dim(
        jnp.zeros_like(gain_zero), gain_own_part, tm * width, axis=0
    )
    gain_grads = lax.psum(
        jnp.stack([grad_gain_zero + own_gain, grad_gain_one, grad_gain_two]),
        ("series", "tm"),
    )
    gain_grads = lax.dynamic_slice_in_dim(gain_grads, tm * width, width, axis=1)
    return (
        output,
        input_grad,
        grad_downs[0],
        grad_downs[1],
        grad_ups[0],
        grad_ups[1],
        grad_isos[0],
        grad_isos[1],
        weight_grads[0].astype(f32),
        weight_grads[1].astype(f32),
        weight_grads[2].astype(f32),
        gain_grads[0],
        gain_grads[1],
        gain_grads[2],
        grad_regress,
    )


def solution(mesh):
    return jax.shard_map(
        shards,
        mesh=mesh,
        in_specs=(
            P("series", "tm", None),
            P("series", "tm", None),
            P("series"),
            P(None, None, "tm"),
            P(None, None, "tm"),
            P(None, None, "tm"),
            P(None, None, "tm"),
            P(None, None, "tm"),
            P(None, None, "tm"),
            P(None, None, "tm"),
            P(None, "tm"),
            P(None, "tm"),
            P("tm"),
            P("tm"),
            P("tm"),
            P("tm", None),
        ),
        out_specs=(
            P("series", "tm", None),
            P("series", "tm", None),
            P(None, "series", "tm"),
            P(None, "series", "tm"),
            P(None, "series", "tm"),
            P(None, "series", "tm"),
            P(None, "series", "tm"),
            P(None, "series", "tm"),
            P(None, None, "tm"),
            P(None, "tm"),
            P(None, "tm"),
            P("tm"),
            P("tm"),
            P("tm"),
            P("tm", None),
        ),
        check_vma=False,
    )
```

time: 2260 us -> 888 us (0.39)
  waiting for transfers between devices: 1530 us -> 212 us
  matrix products: 235 us -> 134 us
  blocking collectives: 174 us -> 84 us
  local copies, waits for them, and re-layouts: 228 us -> 288 us
  other arithmetic: 38.9 us -> 82.9 us
  Pallas kernels: 0 us -> 31.5 us
    reduce_scatter x10 -> x5, waiting for transfers between devices: 1160 us -> 40.1 us  [the longest x1 40 us: shards(): lax.psum_scatter(frames_partial.astype(bf16), 'tm', scatter_dimension=1,...]
    all_gather x7 -> x6, waiting for transfers between devices: 165 us -> 23.7 us  [the longest x1 23.7 us: shards(): inputs_all = lax.all_gather(inputs, 'tm', axis=1, tiled=True)]
    dot_general x37 -> x27, matrix products: 235 us -> 113 us  [dot32(): return jnp.einsum(spec, a, b, preferred_element_type=f32)]
    unnamed x29 -> x17, waiting for transfers between devices: 106 us -> 3.44 us
    psum x1, blocking collectives: 138 us -> 39.8 us  [shards(): lax.psum(jnp.stack([grad_gain_zero + own_gain, grad_gain_one, grad_gain_t...]
    all_to_all x4 -> x7, waiting for transfers between devices: 1.5 us -> 73.5 us  [the longest x1 20.7 us: to_time(): moved = lax.all_to_all(parts, 'tm', split_axis=0, concat_axis=0, tiled=True)]
    unnamed x207 -> x204, local copies, waits for them, and re-layouts: 130 us -> 78.7 us
    transpose x2 -> x9, local copies, waits for them, and re-layouts: 52.1 us -> 8.95 us  [the longest x2 3.27 us: to_time(): block.reshape(series, count, length // count, width).transpose(1, 0, 2, 3)]
  transfers between devices with their start and end apart: 30 -> 22, of which waited for: 21 -> 9; matrix products, arithmetic and copies ran while one was open for 19% -> 51% of each run, Pallas kernels for 0% -> 4%
where the time goes in v1:
time: 888 us; the launch traced here: 880 us
  local copies, waits for them, and re-layouts  288 us (32%)
  waiting for transfers between devices  212 us (24%)
  matrix products  134 us (15%)
  blocking collectives  84 us (9%)
  other arithmetic  82.9 us (9%)
  starting transfers between devices  32.8 us (4%)
  Pallas kernels  31.5 us (4%)
  between operations  15.5 us (2%)
    dot_general x27, matrix products, dot32(): return jnp.einsum(spec, a, b, preferred_element_type=f32)  113 us
    unnamed x204, local copies, waits for them, and re-layouts  78.7 us
    psum x1, waiting for transfers between devices, shards(): weight_grads = lax.psum(weight_grads, 'series')  70.9 us
    dot_general x6, local copies, waits for them, and re-layouts, dot32(): return jnp.einsum(spec, a, b, preferred_element_type=f32)  40.7 us
    reduce_scatter x1, waiting for transfers between devices, shards(): lax.psum_scatter(frames_partial.astype(bf16), 'tm', scatter_dimension=1,...  40 us
    psum x1, blocking collectives, shards(): lax.psum(jnp.stack([grad_gain_zero + own_gain, grad_gain_one, grad_gain_t...  39.8 us
    another operation x4, local copies, waits for them, and re-layouts, iso_kernel_grad(): jnp.stack([source[SHIFTS - p:SHIFTS - p + lag_count] for p in range(SHIFT...  30 us
    reshape x2, local copies, waits for them, and re-layouts, iso_kernel_grad(): stacked = stacked.reshape(lag_count * series, SHIFTS * part)  27.3 us
  transfers between devices with their start and end apart: 22, of which 9 were waited for; matrix products, arithmetic and copies ran while one was open for 51% of the time, Pallas kernels for 4%

profile of v1, /device:TPU:0, one launch (start us, length us, event | category | flops | bytes accessed | tf_op | source)
XLA Modules:
  0.0 879.8 jit_solution(6698162304395877299)
XLA Ops:
  22.8 23.7 %all-gather.8.cloned.1.call-done = bf16[3,1344,512]{2,1,0:T(8,128)(2,1)} async-done(((bf16[3,336,512]{2,1,0:T(8,128)(2,1)}), bf16[3,1344,512]{2,1,0:T(8,128)(2,1)}) %all-gather.8.cloned.1.call-update) | async-done | bytes 4128784 | tf_op jit(solution)/shard_map/all_gather | solution.py:246
  46.5 9.5 %fusion.13 = f32[3,112,128]{2,0,1:T(4,128)S(1)} fusion(bf16[12,512,128]{2,1,0:T(8,128)(2,1)} %param.19, bf16[3,1344,512]{2,1,0:T(8,128)(2,1)} %all-gather.8.cloned.1.call-done), kind=kOutput, calls=%fused_computation.17 | convolution fusion | flops 526123008 | bytes 5873664 | tf_op jit(solution)/shard_map/conv_general_dilated | solution.py:280
  56.0 10.9 %fusion.11 = f32[3,84,128]{2,0,1:T(4,128)S(1)} fusion(bf16[16,512,128]{2,1,0:T(8,128)(2,1)S(1)} %copy-done, bf16[3,1344,512]{2,1,0:T(8,128)(2,1)} %all-gather.8.cloned.1.call-done), kind=kOutput, calls=%fused_computation.15 | convolution fusion | flops 525336576 | bytes 6354944 | tf_op jit(solution)/shard_map/conv_general_dilated | solution.py:280
  86.1 11.2 %shard_map.271 = f32[3,112,128]{2,1,0:T(8,128)S(1)} custom-call(bf16[336,512]{1,0:T(8,128)(2,1)S(1)} %bitcast.427, bf16[112,512,128]{2,1,0:T(8,128)(2,1)} %kernel_ref.6), custom_call_target="tpu_custom_call" | custom-call | flops 4932501504 | bytes 14680064 | tf_op jit(solution)/shard_map/pallas_call | solution.py:85
  98.0 11.3 %all_gather.35 = bf16[4,588,128]{2,1,0:T(8,128)(2,1)S(1)} all-gather(bf16[1,588,128]{2,1,0:T(8,128)(2,1)S(1)} %convert_element_type.316), channel_id=1, replica_groups=mesh['series'=8,'tm'=4] {'tm'}, dimensions={0}, use_global_device_ids=true | all-gather | bytes 752640 | tf_op jit(solution)/shard_map/all_gather | solution.py:189
  112.8 8.4 multiply_reduce_fusion.17
  144.1 20.7 %all-to-all-done = bf16[4,3,336,128]{3,2,1,0:T(8,128)(2,1)} async-done(((bf16[4,3,336,128]{3,2,1,0:T(8,128)(2,1)}), bf16[4,3,336,128]{3,2,1,0:T(8,128)(2,1)}, u32[]{:S(2)}, u32[]{:S(2)}) %all-to-all-start) | async-done | bytes 1032224 | tf_op jit(solution)/shard_map/all_to_all | solution.py:174
  164.9 19.0 %all_to_all.66 = bf16[4,3,336,128]{3,2,1,0:T(8,128)(2,1)S(1)} all-to-all(bf16[4,3,336,128]{3,2,1,0:T(8,128)(2,1)} %copy.239), channel_id=1, replica_groups=mesh['series'=8,'tm'=4] {'tm'}, dimensions={0} | all-to-all | bytes 2064384 | tf_op jit(solution)/shard_map/all_to_all | solution.py:174
  220.2 9.5 %fusion.8 = bf16[1008,2048]{1,0:T(8,128)(2,1)S(1)} fusion(f32[1008,2048]{1,0:T(8,128)} %fusion.99, bf16[2048,512]{1,0:T(8,128)(2,1)S(1)} %copy-done.72, f32[1008,512]{1,0:T(8,128)S(1)} %get-tuple-element.131), kind=kOutput, calls=%fused_computation.10 | convolution fusion | flops 2155732992 | bytes 16547840 | tf_op jit(solution)/shard_map/rd,fd->rf/dot_general | solution.py:19
  243.5 8.9 %convolution_convert_fusion.1 = bf16[2048,512]{1,0:T(8,128)(2,1)} fusion(f32[1008,512]{1,0:T(8,128)} %copy-done.36, f32[1008,2048]{1,0:T(8,128)} %fusion.99), kind=kOutput, calls=%fused_computation.27 | convolution fusion | flops 2134073344 | bytes 12419072 | tf_op jit(solution)/shard_map/rf,rd->fd/dot_general | solution.py:19
  301.3 11.3 %all-to-all-done.3 = bf16[4,3,336,128]{3,2,1,0:T(8,128)(2,1)} async-done(((bf16[4,3,336,128]{3,2,1,0:T(8,128)(2,1)}), bf16[4,3,336,128]{3,2,1,0:T(8,128)(2,1)}, u32[]{:S(2)}, u32[]{:S(2)}) %all-to-all-start.3) | async-done | bytes 1032224 | tf_op jit(solution)/shard_map/all_to_all | solution.py:182
  321.6 11.2 %convert_bitcast_fusion.5 = (bf16[4,588,128]{2,0,1:T(4,128)(2,1)}, f32[588]{0:T(1024)S(1)}) fusion(f32[588,4,128]{2,1,0:T(4,128)} %reshape.453, f32[588]{0:T(1024)S(1)} %add_rsqrt_fusion.4, f32[588,4,128]{2,1,0:T(4,128)S(1)} %get-tuple-element.127, f32[588]{0:T(1024)S(1)} %broadcast_multiply_fusion.12, f32[4,128]{1,0:T(4,128)S(1)} %bitcast.481), kind=kLoop, calls=%fused_computation.150 | loop fusion | flops 1805748 | bytes 3019664 | tf_op jit(solution)/shard_map/transpose | solution.py:197
  341.0 11.7 %all-to-all-done.4 = bf16[4,608,128]{2,1,0:T(8,128)(2,1)} async-done(((bf16[4,608,128]{2,1,0:T(8,128)(2,1)}), bf16[4,608,128]{2,1,0:T(8,128)(2,1)}, u32[]{:S(2)}, u32[]{:S(2)}) %all-to-all-start.4) | async-done | bytes 622624 | tf_op jit(solution)/shard_map/all_to_all | solution.py:209
  382.1 9.5 %copy.251 = bf16[3,1344,512]{1,0,2:T(4,128)(2,1)} copy(bf16[3,1344,512]{2,1,0:T(8,128)(2,1)} %all-gather.8.cloned.1.call-done) | data formatting | bytes 8257536 | tf_op jit(solution)/shard_map/all_gather | solution.py:246
  391.7 20.1 %all-to-all-done.7 = bf16[3,196,512]{1,0,2:T(4,128)(2,1)S(1)} async-done(((bf16[3,196,512]{1,0,2:T(4,128)(2,1)}), bf16[3,196,512]{1,0,2:T(4,128)(2,1)S(1)}, u32[]{:S(2)}, u32[]{:S(2)}) %all-to-all-start.7) | async-done | bytes 602144 | tf_op jit(solution)/shard_map/all_to_all | solution.py:293
  424.8 10.6 %shard_map.273 = f32[336,512]{1,0:T(8,128)S(1)} custom-call(f32[3,224,128]{2,1,0:T(8,128)S(1)} %pad_convert_fusion.grad_ref, bf16[112,512,128]{2,1,0:T(8,128)(2,1)} %kernel_ref.6), custom_call_target="tpu_custom_call" | custom-call | flops 4932501504 | bytes 14680064 | tf_op jit(solution)/shard_map/pallas_call | solution.py:131
  490.0 10.7 %copy.268 = bf16[84,24,16,64]{3,2,1,0:T(8,128)(2,1)} copy(bf16[84,24,16,64]{0,3,1,2:T(8,128)(2,1)} %bitcast_dynamic-update-slice_fusion.4) | data formatting | bytes 8257536 | tf_op jit(solution)/shard_map/stack | solution.py:156
  500.7 11.8 %reshape.468 = bf16[2016,1024]{1,0:T(8,128)(2,1)} reshape(bf16[84,24,16,64]{3,2,1,0:T(8,128)(2,1)} %copy.268) | data formatting | bytes 8257536 | tf_op jit(solution)/shard_map/reshape | solution.py:159
  521.7 9.0 %copy.249 = f32[3,112,12,512]{3,2,1,0:T(8,128)} copy(f32[3,112,12,512]{3,1,2,0:T(8,128)S(1)} %fusion.28) | data formatting | bytes 16515072 | tf_op jit(solution)/shard_map/smo,kco->smkc/dot_general | solution.py:19
  530.7 11.0 %reshape.461 = f32[3,1344,512]{2,1,0:T(8,128)} reshape(f32[3,112,12,512]{3,2,1,0:T(8,128)} %copy.249) | data formatting | bytes 16515072 | tf_op jit(solution)/shard_map/reshape | solution.py:410
  541.7 8.1 slice.333
  560.0 9.3 %add_convert_fusion = bf16[3,1344,512]{2,1,0:T(8,128)(2,1)} fusion(f32[3,1336,512]{2,1,0:T(8,128)} %slice.335, f32[3,1338,512]{2,1,0:T(8,128)} %slice.333), kind=kLoop, calls=%fused_computation.13 | loop fusion | flops 4128768 | bytes 20557824 | tf_op jit(solution)/shard_map/convert_element_type | solution.py:415
  574.1 17.4 %copy.263 = bf16[112,24,16,64]{3,2,1,0:T(8,128)(2,1)} copy(bf16[112,24,16,64]{0,3,1,2:T(8,128)(2,1)} %bitcast_dynamic-update-slice_fusion.19) | data formatting | bytes 11010048 | tf_op jit(solution)/shard_map/stack | solution.py:156
  591.5 15.6 %reshape.465 = bf16[2688,1024]{1,0:T(8,128)(2,1)} reshape(bf16[112,24,16,64]{3,2,1,0:T(8,128)(2,1)} %copy.263) | data formatting | bytes 11010048 | tf_op jit(solution)/shard_map/reshape | solution.py:159
  607.1 8.2 copy.264
  615.4 39.8 %psum.38 = f32[3,512]{1,0:T(4,128)S(1)} all-reduce(f32[3,512]{1,0:T(4,128)S(1)} %pad_maximum_fusion.4), channel_id=1, replica_groups=mesh['series'=8,'tm'=4] {'series','tm'}, use_global_device_ids=true, to_apply=%region_37.38 | all-reduce | flops 1536 | bytes 12288 | tf_op jit(solution)/shard_map/psum | solution.py:434
  691.2 9.5 %convolution_bitcast_fusion.1 = f32[7,16,64,128]{3,2,0,1:T(8,128)S(1)} fusion(bf16[16,64,2688,1]{2,1,3,0:T(8,128)(2,1)} %bitcast.447, bf16[7,128,2688,1]{2,1,0,3:T(8,128)(2,1)} %bitcast.449), kind=kOutput, calls=%fused_computation.82 | convolution fusion | flops 4932501504 | bytes 13991936 | tf_op jit(solution)/shard_map/ra,rb->ab/dot_general | solution.py:19
  715.2 8.7 copy.256
  724.0 11.2 %copy.254 = bf16[24,1344,64]{2,0,1:T(8,128)(2,1)} copy(bf16[24,1344,64]{1,2,0:T(8,128)(2,1)} %get-tuple-element.130) | data formatting | bytes 8257536 | tf_op jit(solution)/shard_map/slice | solution.py:426
  735.2 8.8 %fusion.46 = f32[12,64,128]{2,1,0:T(8,128)} fusion(bf16[24,112,12,64]{3,0,2,1:T(8,128)(2,1)} %bitcast.441, bf16[24,196,128]{2,1,0:T(8,128)(2,1)} %all-gather.18.cloned.1.call-done), kind=kOutput, calls=%fused_computation.123 | convolution fusion | flops 528482304 | bytes 9338880 | tf_op jit(solution)/shard_map/smkc,smo->kco/dot_general | solution.py:19
  751.2 70.9 %all-reduce.15.cloned.1.call-done = (bf16[2,512,128]{2,1,0:T(8,128)(2,1)}, bf16[512,512]{1,0:T(8,128)(2,1)}, bf16[2048,128]{1,0:T(8,128)(2,1)}, bf16[336,1344]{1,0:T(8,128)(2,1)}) async-done(((bf16[2,512,128]{2,1,0:T(8,128)(2,1)}, bf16[512,512]{1,0:T(8,128)(2,1)}, bf16[2048,128]{1,0:T(8,128)(2,1)}, bf16[336,1344]{1,0:T(8,128)(2,1)}), (bf16[2,512,128]{2,1,0:T(8,128)(2,1)}, bf16[512,512]{1,0:T(8,128)(2,1)}, ...) | async-done | bytes 2213904 | tf_op jit(solution)/shard_map/psum | solution.py:352
  827.8 40.0 %reduce-scatter.14.cloned.1.call-done = bf16[3,336,512]{2,1,0:T(8,128)(2,1)} async-done(((bf16[3,1344,512]{2,1,0:T(8,128)(2,1)}), bf16[3,336,512]{2,1,0:T(8,128)(2,1)}) %reduce-scatter.14.cloned.1.call-update) | async-done | bytes 1032208 | tf_op jit(solution)/shard_map/reduce_scatter | solution.py:414
  (420 shorter events, 366.7 us)
Async XLA Ops:
  7.2 48.8 %copy-start = (bf16[16,512,128]{2,1,0:T(8,128)(2,1)S(1)}, bf16[16,512,128]{2,1,0:T(8,128)(2,1)}, u32[]{:S(2)}) copy-start(bf16[16,512,128]{2,1,0:T(8,128)(2,1)} %param.20) | copy-start | bytes 6291460
  7.2 39.2 %all-gather.8.cloned.1.call-start = ((), (), s32[]{:S(2)}) async-start(), calls=%async_computation.15 | async-start | bytes 5160960 | tf_op jit(solution)/shard_map/all_gather | solution.py:246
  8.0 181.6 %all-gather.10.cloned.1.call-start = ((), (), s32[]{:S(2)}) async-start(), calls=%async_computation.16 | async-start | bytes 1310720 | tf_op jit(solution)/shard_map/all_gather | solution.py:249
  8.7 185.6 %all-gather.12.cloned.1.call-start = ((), (), s32[]{:S(2)}) async-start(), calls=%async_computation.17 | async-start | bytes 2621440 | tf_op jit(solution)/shard_map/all_gather | solution.py:250
  9.4 192.7 %all-gather.14.cloned.1.call-start = ((), (), s32[]{:S(2)}) async-start(), calls=%async_computation.18 | async-start | bytes 2621440 | tf_op jit(solution)/shard_map/all_gather | solution.py:251
  10.0 200.7 %reduce-scatter.12.cloned.1.call-start = ((), (), s32[]{:S(2)}) async-start(), calls=%async_computation.20 | async-start | bytes 5160960 | tf_op jit(solution)/shard_map/reduce_scatter | solution.py:261
  22.8 316.9 %copy-start.54 = (f32[1,512]{1,0:T(1,128)}, f32[1,512]{1,0:T(1,128)S(1)}, u32[]{:S(2)}) copy-start(f32[1,512]{1,0:T(1,128)S(1)} %get-tuple-element.148) | copy-start | bytes 6148
  134.8 30.0 %all-to-all-start = ((bf16[4,3,336,128]{3,2,1,0:T(8,128)(2,1)}), bf16[4,3,336,128]{3,2,1,0:T(8,128)(2,1)}, u32[]{:S(2)}, u32[]{:S(2)}) async-start(bf16[4,3,336,128]{3,2,1,0:T(8,128)(2,1)} %copy.236), calls=%async_computation | async-start | bytes 2064384 | tf_op jit(solution)/shard_map/all_to_all | solution.py:174
  139.1 333.8 %reduce-scatter.22.cloned.1.call-start = ((), (), s32[]{:S(2)}) async-start(), calls=%async_computation.27 | async-start | bytes 1310720
  185.9 91.9 %copy-start.48 = (f32[3,336]{1,0:T(4,128)}, f32[3,336]{1,0:T(4,128)S(1)}, u32[]{:S(2)}) copy-start(f32[3,336]{1,0:T(4,128)S(1)} %broadcast_multiply_fusion.5) | copy-start | bytes 12100
  185.9 75.4 %copy-start.52 = (f32[3,336]{1,0:T(4,128)}, f32[3,336]{1,0:T(4,128)S(1)}, u32[]{:S(2)}) copy-start(f32[3,336]{1,0:T(4,128)S(1)} %broadcast_multiply_fusion.6) | copy-start | bytes 12100
  186.8 91.0 %copy-start.50 = (f32[3,336]{1,0:T(4,128)}, f32[3,336]{1,0:T(4,128)S(1)}, u32[]{:S(2)}) copy-start(f32[3,336]{1,0:T(4,128)S(1)} %add_rsqrt_fusion) | copy-start | bytes 12100
  187.8 73.6 %copy-start.56 = (f32[3,336]{1,0:T(4,128)}, f32[3,336]{1,0:T(4,128)S(1)}, u32[]{:S(2)}) copy-start(f32[3,336]{1,0:T(4,128)S(1)} %add_rsqrt_fusion.1) | copy-start | bytes 12100
  243.5 231.5 %reduce-scatter.24.cloned.1.call-start = ((), (), s32[]{:S(2)}) async-start(), calls=%async_computation.28 | async-start | bytes 2621440
  256.4 220.7 %all-gather.16.cloned.1.call-start = ((), (), s32[]{:S(2)}) async-start(), calls=%async_computation.19 | async-start | bytes 5160960 | tf_op jit(solution)/shard_map/all_gather | solution.py:326
  266.6 18.6 %all-to-all-start.2 = ((bf16[4,3,336,128]{3,2,1,0:T(8,128)(2,1)}), bf16[4,3,336,128]{3,2,1,0:T(8,128)(2,1)}, u32[]{:S(2)}, u32[]{:S(2)}) async-start(bf16[4,3,336,128]{3,2,1,0:T(8,128)(2,1)} %bitcast.460), calls=%async_computation.3 | async-start | bytes 2064384 | tf_op jit(solution)/shard_map/all_to_all | solution.py:182
  270.8 211.4 %reduce-scatter.20.cloned.1.call-start = ((), (), s32[]{:S(2)}) async-start(), calls=%async_computation.26 | async-start | bytes 2621440 | tf_op jit(solution)/shard_map/reduce_scatter | solution.py:349
  285.2 27.4 %all-to-all-start.3 = ((bf16[4,3,336,128]{3,2,1,0:T(8,128)(2,1)}), bf16[4,3,336,128]{3,2,1,0:T(8,128)(2,1)}, u32[]{:S(2)}, u32[]{:S(2)}) async-start(bf16[4,3,336,128]{3,2,1,0:T(8,128)(2,1)} %bitcast_bitcast_fusion.2), calls=%async_computation.4 | async-start | bytes 2064384 | tf_op jit(solution)/shard_map/all_to_all | solution.py:182
  335.4 17.3 %all-to-all-start.4 = ((bf16[4,608,128]{2,1,0:T(8,128)(2,1)}), bf16[4,608,128]{2,1,0:T(8,128)(2,1)}, u32[]{:S(2)}, u32[]{:S(2)}) async-start(bf16[4,608,128]{2,1,0:T(8,128)(2,1)} %copy.247), calls=%async_computation.5 | async-start | bytes 1245184 | tf_op jit(solution)/shard_map/all_to_all | solution.py:209
  339.6 316.1 %all-gather.20.cloned.1.call-start = ((), (), s32[]{:S(2)}) async-start(), calls=%async_computation.25 | async-start | bytes 1382400 | tf_op jit(solution)/shard_map/all_gather | solution.py:393
  356.7 346.2 %reduce-scatter.16.cloned.1.call-start = ((), (), s32[]{:S(2)}) async-start(), calls=%async_computation.23 | async-start | bytes 2359296 | tf_op jit(solution)/shard_map/reduce_scatter | solution.py:369
  364.5 340.1 %reduce-scatter.18.cloned.1.call-start = ((), (), s32[]{:S(2)}) async-start(), calls=%async_computation.24 | async-start | bytes 2359296 | tf_op jit(solution)/shard_map/reduce_scatter | solution.py:369
  375.9 35.9 %all-to-all-start.7 = ((bf16[3,196,512]{1,0,2:T(4,128)(2,1)}), bf16[3,196,512]{1,0,2:T(4,128)(2,1)S(1)}, u32[]{:S(2)}, u32[]{:S(2)}) async-start(bf16[3,196,512]{1,0,2:T(4,128)(2,1)} %copy.260), calls=%async_computation.11 | async-start | bytes 2097152 | tf_op jit(solution)/shard_map/all_to_all | solution.py:293
  440.4 14.0 %all-to-all-start.5 = ((bf16[4,588,128]{2,1,0:T(8,128)(2,1)}), bf16[4,588,128]{2,1,0:T(8,128)(2,1)}, u32[]{:S(2)}, u32[]{:S(2)}) async-start(bf16[4,588,128]{2,1,0:T(8,128)(2,1)} %copy.248), calls=%async_computation.6 | async-start | bytes 1212416 | tf_op jit(solution)/shard_map/all_to_all | solution.py:209
  454.4 252.0 %all-to-all-start.6 = ((bf16[3,1344,512]{1,0,2:T(4,128)(2,1)}), bf16[3,1344,512]{1,0,2:T(4,128)(2,1)}, u32[]{:S(2)}, u32[]{:S(2)}) async-start(bf16[3,1344,512]{1,0,2:T(4,128)(2,1)} %copy.251), calls=%async_computation.8 | async-start | bytes 11534336 | tf_op jit(solution)/shard_map/all_to_all | solution.py:253
  459.1 276.1 %all-gather.18.cloned.1.call-start = ((), (), s32[]{:S(2)}) async-start(), calls=%async_computation.22 | async-start | bytes 1382400 | tf_op jit(solution)/shard_map/all_gather | solution.py:402
  462.6 359.5 %all-reduce.15.cloned.1.call-start = ((), (), s32[]{:S(2)}) async-start(), calls=%async_computation.29 | async-start | bytes 4513792 | tf_op jit(solution)/shard_map/psum | solution.py:352
  482.3 385.5 %reduce-scatter.14.cloned.1.call-start = ((), (), s32[]{:S(2)}) async-start(), calls=%async_computation.21 | async-start | bytes 5160960 | tf_op jit(solution)/shard_map/reduce_scatter | solution.py:414
  824.7 43.1 %copy-start.49 = (f32[3,336]{1,0:T(4,128)S(1)}, f32[3,336]{1,0:T(4,128)}, u32[]{:S(2)}) copy-start(f32[3,336]{1,0:T(4,128)} %copy-done.48) | copy-start | bytes 12100
  824.7 43.1 %copy-start.51 = (f32[3,336]{1,0:T(4,128)S(1)}, f32[3,336]{1,0:T(4,128)}, u32[]{:S(2)}) copy-start(f32[3,336]{1,0:T(4,128)} %copy-done.50) | copy-start | bytes 12100
  824.7 43.1 %copy-start.53 = (f32[3,336]{1,0:T(4,128)S(1)}, f32[3,336]{1,0:T(4,128)}, u32[]{:S(2)}) copy-start(f32[3,336]{1,0:T(4,128)} %copy-done.52) | copy-start | bytes 12100
  824.8 43.1 %copy-start.55 = (f32[1,512]{1,0:T(1,128)S(1)}, f32[1,512]{1,0:T(1,128)}, u32[]{:S(2)}) copy-start(f32[1,512]{1,0:T(1,128)} %copy-done.54) | copy-start | bytes 6148
  (65 other events, 450.8 us)
Sparse Core Ops, SparseCore 0:
  9.6 36.8 all-gather.7
  48.0 16.8 all-gather.9
  66.5 22.5 all-gather.11
  90.5 26.0 all-gather.13
  119.1 55.9 reduce-scatter.11
  243.6 24.8 reduce-scatter.21
  271.1 40.2 reduce-scatter.23
  313.0 37.6 all-gather.15
  353.4 31.7 reduce-scatter.19
  387.8 44.9 all-gather.19
  436.3 143.6 reduce-scatter.15
  583.3 84.1 reduce-scatter.17
  670.2 40.4 all-gather.17
  715.7 106.3 all-reduce.14
  824.7 43.0 reduce-scatter.13

commit v2 on v1

v2 whole, which is shorter than its diff:
```python
import functools

import jax
import jax.numpy as jnp
from jax import lax
from jax.experimental import pallas as pl
from jax.experimental.pallas import tpu as pltpu
from jax.sharding import PartitionSpec as P

LEN = 1344
SHIFTS = 16
TAPS = 4

epsilon = 1e-05
bf16 = jnp.bfloat16
f32 = jnp.float32

GELU_A = 0.7978845608028654
GELU_B = 0.044715


def dot32(spec, a, b):
    return jnp.einsum(spec, a, b, preferred_element_type=f32)


def matmul(a, b):
    return jnp.dot(a, b, preferred_element_type=f32)


def matmul_nt(a, b):
    return lax.dot_general(a, b, (((1,), (1,)), ((), ())), preferred_element_type=f32)


def matmul_tn(a, b):
    return lax.dot_general(a, b, (((0,), (0,)), ((), ())), preferred_element_type=f32)


def norm_parts(field):
    centred = field - jnp.mean(field, axis=-1, keepdims=True)
    spread = jnp.mean(centred * centred, axis=-1, keepdims=True)
    scale = lax.rsqrt(spread + epsilon)
    return centred * scale, scale


def norm_back(unit, scale, gain, upstream):
    lifted = gain * upstream
    mean_lift = jnp.mean(lifted, axis=-1, keepdims=True)
    mean_both = jnp.mean(lifted * unit, axis=-1, keepdims=True)
    gain_grad = jnp.sum(upstream * unit, axis=0, keepdims=True)
    return (lifted - mean_lift - unit * mean_both) * scale, gain_grad


def gelu_forward(h):
    return 0.5 * h * (1.0 + jnp.tanh(GELU_A * (h + GELU_B * (h * h * h))))


def gelu_slope(h):
    square = h * h
    t = jnp.tanh(GELU_A * (h + GELU_B * (square * h)))
    return 0.5 * (1.0 + t) + 0.5 * h * (1.0 - t * t) * GELU_A * (1.0 + 3.0 * GELU_B * square)


def padded_rows(count):
    return -(-count // 16) * 16


def lag_block(count):
    return max(n for n in range(2, 15, 2) if count % n == 0)


def whole_block(shape):
    return pl.BlockSpec(shape, lambda *_: (0,) * len(shape))


def kernel_call(body, grid, in_specs, out_specs, out_shape, scratch, flops, moved):
    return pl.pallas_call(
        body,
        grid=grid,
        in_specs=in_specs,
        out_specs=out_specs,
        out_shape=out_shape,
        scratch_shapes=scratch,
        compiler_params=pltpu.CompilerParams(vmem_limit_bytes=60 * 2**20),
        cost_estimate=pl.CostEstimate(flops=flops, bytes_accessed=moved, transcendentals=0),
    )


class Sizes:
    def __init__(self, series, length, features, count, strides):
        self.series = series
        self.length = length
        self.features = features
        self.count = count
        self.width = features // count
        self.whole = length * count
        self.strides = strides
        self.rows = tuple(self.whole // k for k in strides)
        self.padded = tuple(padded_rows(m) for m in self.rows)
        self.starts = (0, self.padded[0])
        self.packed = sum(self.padded)


def lane_block(index, width):
    return pl.ds(pl.multiple_of(index * width, width), width)


def place_rows(sizes, n, tm, refs, target_ref):
    first, rows = sizes.starts[n], sizes.padded[n]
    for m, ref in enumerate(refs):
        for s in range(sizes.series):
            target_ref[s * rows : (s + 1) * rows, lane_block(tm ^ m, sizes.width)] = ref[
                s, first : first + rows, :
            ].astype(target_ref.dtype)


SCALAR = pl.BlockSpec(memory_space=pltpu.SMEM)


def row_mask(sizes, n, columns):
    row = lax.broadcasted_iota(jnp.int32, (sizes.padded[n], columns), 0)
    return row < sizes.rows[n]


def down_body(sizes, groups, tm_ref, *refs):
    x_refs = refs[: sizes.count]
    down_a_ref, down_b_ref, tanh_ref, coarse_ref, sent_ref, steps_ref = refs[sizes.count :]
    head = 8
    tiles, extent, lanes = steps_ref.shape
    tail = extent - head - sizes.whole
    for c in range(tiles):
        steps_ref[c, 0:head, :] = jnp.zeros((head, lanes), f32)
        steps_ref[c, head + sizes.whole :, :] = jnp.zeros((tail, lanes), f32)
        for m, x_ref in enumerate(x_refs):
            place = pl.multiple_of(head + (tm_ref[0] ^ m) * sizes.length, 8)
            steps_ref[c, pl.ds(place, sizes.length), :] = x_ref[
                0, :, c * lanes : (c + 1) * lanes
            ].astype(f32)
    for n, down_ref in enumerate((down_a_ref, down_b_ref)):
        stride, rows = sizes.strides[n], sizes.padded[n]
        total = jnp.zeros((rows, sizes.width), f32)
        for r in range(0, stride, 2):
            taps = [
                steps_ref[c, pl.ds(head - stride // 2 + r + e, rows, stride=stride), :]
                for e in range(2)
                for c in range(tiles)
            ]
            frames = jnp.concatenate(taps, axis=1).astype(bf16)
            total += matmul(frames, jnp.concatenate([down_ref[r], down_ref[r + 1]], axis=0))
        value = jnp.where(row_mask(sizes, n, sizes.width), jnp.tanh(total), 0.0)
        place = slice(sizes.starts[n], sizes.starts[n] + rows)
        tanh_ref[0, place, :] = value
        coarse_ref[0, place, :] = value.astype(bf16)
    if groups * 2 == tiles * 4:
        half, extra = sizes.whole // 2, sent_ref.shape[2]
        for c in range(tiles):
            early = steps_ref[c, 0:extra, :]
            late = steps_ref[c, half : half + extra, :]
            low = lax.broadcasted_iota(jnp.int32, early.shape, 1) < lanes // 2
            early_turned = pltpu.roll(early, lanes // 2, axis=1)
            late_turned = pltpu.roll(late, lanes // 2, axis=1)
            sent_ref[2 * c, 0] = jnp.where(low, early, late_turned).astype(bf16)
            sent_ref[2 * c + 1, 0] = jnp.where(low, early_turned, late).astype(bf16)


def down_forward(sizes, groups, tm, pieces, down_a, down_b):
    extent = 8 + max(k * m for k, m in zip(sizes.strides, sizes.padded)) + 16
    packed = (sizes.series, sizes.packed, sizes.width)
    block = pl.BlockSpec((1, sizes.packed, sizes.width), lambda s: (s, 0, 0))
    row_block = pl.BlockSpec((1, sizes.length, sizes.features), lambda s: (s, 0, 0))
    extra = 8 + sizes.whole // 2
    sent = (groups if groups == 8 else 1, sizes.series, extra, 128)
    return kernel_call(
        functools.partial(down_body, sizes, groups),
        (sizes.series,),
        [SCALAR]
        + [row_block] * sizes.count
        + [whole_block(down_a.shape), whole_block(down_b.shape)],
        [block, block, pl.BlockSpec((sent[0], 1, extra, 128), lambda s: (0, s, 0, 0))],
        [
            jax.ShapeDtypeStruct(packed, f32),
            jax.ShapeDtypeStruct(packed, bf16),
            jax.ShapeDtypeStruct(sent, bf16),
        ],
        [pltpu.VMEM((sizes.features // 128, extent, 128), f32)],
        4 * sizes.series * sizes.whole * sizes.features * sizes.width,
        2 * (pieces[0].size * 8 + down_a.size + down_b.size),
    )(tm, *pieces, down_a, down_b)


def iso_body(sizes, lags, steps, tm_ref, *refs):
    piece_refs = refs[: sizes.count]
    iso_a_ref, iso_b_ref, tanh_ref, mixed_ref = refs[sizes.count : sizes.count + 4]
    scratch = refs[sizes.count + 4 :]
    coarse_refs, total_refs = scratch[:2], scratch[2:]
    step = pl.program_id(0)

    @pl.when(step == 0)
    def start():
        for n in range(2):
            place_rows(sizes, n, tm_ref[0], piece_refs, coarse_refs[n])
            total_refs[n][...] = jnp.zeros_like(total_refs[n])

    def add_lags(n, kernel_ref, first_lag):
        rows, width = sizes.padded[n], sizes.width
        coarse = coarse_refs[n][...]
        for pair in range(lags[n] // 2):
            both = jnp.concatenate([kernel_ref[2 * pair], kernel_ref[2 * pair + 1]], axis=1)
            part = matmul(coarse, both)
            for half in range(2):
                place = pl.ds(first_lag + 2 * pair + half, rows)
                for s in range(sizes.series):
                    total_refs[n][s, place, :] += part[
                        s * rows : (s + 1) * rows, half * width : (half + 1) * width
                    ]

    @pl.when(step < steps[0])
    def first_scale():
        add_lags(0, iso_a_ref, step * lags[0])

    @pl.when(step >= steps[0])
    def second_scale():
        add_lags(1, iso_b_ref, (step - steps[0]) * lags[1])

    @pl.when(step == pl.num_programs(0) - 1)
    def finish():
        for n in range(2):
            mask = row_mask(sizes, n, sizes.width)
            place = slice(sizes.starts[n], sizes.starts[n] + sizes.padded[n])
            for s in range(sizes.series):
                value = jnp.tanh(total_refs[n][s, : sizes.padded[n], :])
                value = jnp.where(mask, value, 0.0)
                tanh_ref[s, place, :] = value
                mixed_ref[s, place, :] = value.astype(bf16)


def iso_steps(sizes):
    lags = tuple(lag_block(m) for m in sizes.rows)
    steps = tuple(m // n for m, n in zip(sizes.rows, lags))
    specs = [
        pl.BlockSpec(
            (lags[0], sizes.features, sizes.width),
            lambda i: (jnp.minimum(i, steps[0] - 1), 0, 0),
        ),
        pl.BlockSpec(
            (lags[1], sizes.features, sizes.width),
            lambda i: (jnp.maximum(i - steps[0], 0), 0, 0),
        ),
    ]
    flops = sum(
        2 * sizes.series * p * m * sizes.features * sizes.width
        for p, m in zip(sizes.padded, sizes.rows)
    )
    return lags, steps, specs, flops


def iso_forward(sizes, tm, coarse_pieces, iso_a, iso_b):
    lags, steps, specs, flops = iso_steps(sizes)
    packed = (sizes.series, sizes.packed, sizes.width)
    return kernel_call(
        functools.partial(iso_body, sizes, lags, steps),
        (sum(steps),),
        [SCALAR] + [whole_block(packed)] * sizes.count + specs,
        [whole_block(packed), whole_block(packed)],
        [jax.ShapeDtypeStruct(packed, f32), jax.ShapeDtypeStruct(packed, bf16)],
        [pltpu.VMEM((sizes.series * p, sizes.features), bf16) for p in sizes.padded]
        + [pltpu.VMEM((sizes.series, 2 * p, sizes.width), f32) for p in sizes.padded],
        flops,
        2 * (iso_a.size + iso_b.size),
    )(tm, *coarse_pieces, iso_a, iso_b)


def tap_specs(sizes, ups):
    steps = tuple(up.shape[0] // TAPS for up in ups)
    block = (TAPS, sizes.features, sizes.width)
    return steps, [
        pl.BlockSpec(block, lambda i: (jnp.minimum(i, steps[0] - 1), 0, 0)),
        pl.BlockSpec(block, lambda i: (jnp.maximum(i - steps[0], 0), 0, 0)),
    ]


def up_body(sizes, steps, tm_ref, *refs):
    count = sizes.count
    coarse_refs, mixed_refs = refs[:count], refs[count : 2 * count]
    gain_ref, up_a_ref, up_b_ref, tanh_ref = refs[2 * count : 2 * count + 4]
    sent_refs = refs[2 * count + 4 : 3 * count + 4]
    sum_refs = refs[3 * count + 4 : 3 * count + 6]
    normed_refs = refs[3 * count + 6 :]
    step = pl.program_id(0)

    def make_normed(n):
        first, rows = sizes.starts[n], sizes.padded[n]
        for m in range(count):
            for s in range(sizes.series):
                total = coarse_refs[m][s, first : first + rows, :].astype(f32)
                total += mixed_refs[m][s, first : first + rows, :].astype(f32)
                sum_refs[n][
                    s * rows : (s + 1) * rows, lane_block(tm_ref[0] ^ m, sizes.width)
                ] = total
        unit, unused = norm_parts(sum_refs[n][...])
        normed_refs[n][...] = (gain_ref[0:1, :] * unit).astype(bf16)

    def taps(n, up_ref, first_tap):
        stride, rows, padded = sizes.strides[n], sizes.rows[n], sizes.padded[n]
        normed = normed_refs[n][...]
        for pair in range(TAPS // 2):
            both = jnp.concatenate([up_ref[2 * pair], up_ref[2 * pair + 1]], axis=1)
            value = jnp.tanh(matmul(normed, both))
            for half in range(2):
                place = pl.ds(first_tap + 2 * pair + half, rows, stride=stride)
                for s in range(sizes.series):
                    tanh_ref[n, s, place, :] = value[
                        s * padded : s * padded + rows,
                        half * sizes.width : (half + 1) * sizes.width,
                    ]

    def send(n):
        for m in range(count):
            place = pl.multiple_of((tm_ref[0] ^ m) * sizes.length, 16)
            for s in range(sizes.series):
                sent_refs[m][n, s] = tanh_ref[n, s, pl.ds(place, sizes.length), :].astype(bf16)

    @pl.when(step == 0)
    def start():
        make_normed(0)
        make_normed(1)

    @pl.when(step < steps[0])
    def first_scale():
        taps(0, up_a_ref, step * TAPS)

    @pl.when(step >= steps[0])
    def second_scale():
        taps(1, up_b_ref, (step - steps[0]) * TAPS)

    @pl.when(step == pl.num_programs(0) - 1)
    def finish():
        send(0)
        send(1)


def up_forward(sizes, tm, coarse_pieces, mixed_pieces, gains, up_a, up_b):
    steps, specs = tap_specs(sizes, (up_a, up_b))
    packed = (sizes.series, sizes.packed, sizes.width)
    wide = (2, sizes.series, sizes.whole, sizes.width)
    sent = (2, sizes.series, sizes.length, sizes.width)
    row_shapes = [(sizes.series * p, sizes.features) for p in sizes.padded]
    outs = kernel_call(
        functools.partial(up_body, sizes, steps),
        (sum(steps),),
        [SCALAR]
        + [whole_block(packed)] * (2 * sizes.count)
        + [whole_block(gains.shape)]
        + specs,
        [whole_block(wide)]
        + [whole_block(sent)] * sizes.count
        + [whole_block(shape) for shape in row_shapes],
        [jax.ShapeDtypeStruct(wide, f32)]
        + [jax.ShapeDtypeStruct(sent, bf16)] * sizes.count
        + [jax.ShapeDtypeStruct(shape, f32) for shape in row_shapes],
        [pltpu.VMEM(shape, bf16) for shape in row_shapes],
        4 * sizes.series * sizes.whole * sizes.features * sizes.width,
        2 * (up_a.size + up_b.size) + 12 * sizes.series * sizes.whole * sizes.width,
    )(tm, *coarse_pieces, *mixed_pieces, gains, up_a, up_b)
    return outs[0], outs[1 : 1 + sizes.count], outs[1 + sizes.count :]


def rows_body(sizes, hidden, held, tm_ref, *refs):
    count = sizes.count
    tanh_refs, refs = refs[:count], refs[count:]
    x_ref, out_grad_ref, back_ref, gains_ref, weights_ref, refs = *refs[:5], refs[5 + held :]
    season_ref, part_ref, refs = *refs[:2], refs[2:]
    sent_refs, grad_refs, refs = refs[:count], refs[count : 2 * count], refs[2 * count :]
    hidden_ref, act_ref, grad_in_ref, grad_out_ref, grad_merge_ref, gain_grads_ref, wide_ref = refs
    step = pl.program_id(0)
    width, features = sizes.width, sizes.features
    chunks = weights_ref.shape[0]
    tiles = hidden // width
    tm = tm_ref[0]
    in_rows = features // chunks
    out_first = tiles * in_rows
    out_rows = hidden * count // chunks
    merge_first = out_first + out_rows
    merge_rows = 2 * features // chunks

    @pl.when(step == 0)
    def start():
        grad_in_ref[...] = jnp.zeros_like(grad_in_ref)
        grad_out_ref[...] = jnp.zeros_like(grad_out_ref)
        grad_merge_ref[...] = jnp.zeros_like(grad_merge_ref)
        gain_grads_ref[...] = jnp.zeros_like(gain_grads_ref)

    gain_zero, gain_one, gain_two = [gains_ref[n : n + 1, :] for n in range(3)]
    wide = x_ref[0].astype(f32)

    def scaled_parts(n):
        for m in range(count):
            wide_ref[n, :, lane_block(tm ^ m, width)] = tanh_refs[m][n, 0].astype(f32)
        return norm_parts(wide_ref[n] + wide)

    def in_full(c):
        return jnp.concatenate(
            [
                jnp.concatenate(
                    [
                        weights_ref[i, c, e * in_rows : (e + 1) * in_rows, :]
                        for e in range(tiles)
                    ],
                    axis=1,
                )
                for i in range(chunks)
            ],
            axis=0,
        )

    def across(chunk, place):
        return jnp.concatenate([weights_ref[chunk, t, place, :] for t in range(count)], axis=1)

    def out_full(c):
        if out_rows > hidden:
            place = pl.ds(pl.multiple_of(out_first + c * hidden, 16), hidden)
            return across(0, place)
        each = hidden // out_rows
        place = slice(out_first, out_first + out_rows)
        return jnp.concatenate([across(c * each + e, place) for e in range(each)], axis=0)

    def merge_full(n):
        if merge_rows > features:
            first = merge_first + n * features
            return across(0, slice(first, first + features))
        each = features // merge_rows
        place = slice(merge_first, merge_first + merge_rows)
        return jnp.concatenate([across(n * each + e, place) for e in range(each)], axis=0)

    units = [scaled_parts(n) for n in range(2)]
    scaled = [(gain_zero * unit).astype(bf16) for unit, unused in units]
    merged = matmul(scaled[0], merge_full(0)) + matmul(scaled[1], merge_full(1))
    unit_one, scale_one = norm_parts(merged)
    first = (gain_one * unit_one).astype(bf16)

    def forward(c, total):
        pre = matmul(first, in_full(c))
        act = gelu_forward(pre).astype(bf16)
        hidden_ref[c] = pre
        act_ref[c] = act
        return total + matmul(act, out_full(c))

    back_proj = lax.fori_loop(0, count, forward, jnp.zeros(merged.shape, f32))
    unit_two, scale_two = norm_parts(first.astype(f32) + back_proj)
    season_ref[0] = (gain_two * unit_two).astype(bf16)

    season_grad = out_grad_ref[0].astype(f32) + back_ref[0].astype(f32)
    sum_grad, gain_grad_two = norm_back(unit_two, scale_two, gain_two, season_grad)
    back_low = sum_grad.astype(bf16)

    def backward(c, total):
        slope = gelu_slope(hidden_ref[c])
        hidden_grad = (matmul_nt(back_low, out_full(c)) * slope).astype(bf16)
        grad_in_ref[c] += matmul_tn(first, hidden_grad)
        grad_out_ref[c] += matmul_tn(act_ref[c], back_low)
        return total + matmul_nt(hidden_grad, in_full(c))

    first_grad = sum_grad + lax.fori_loop(0, count, backward, jnp.zeros(merged.shape, f32))
    merged_grad, gain_grad_one = norm_back(unit_one, scale_one, gain_one, first_grad)
    merged_low = merged_grad.astype(bf16)
    gain_grad_zero = jnp.zeros_like(gain_zero)
    part = jnp.zeros(merged.shape, f32)
    for n in range(2):
        grad_merge_ref[n] += matmul_tn(scaled[n], merged_low)
        unit, scale = units[n]
        sum_part, gain_part = norm_back(
            unit, scale, gain_zero, matmul_nt(merged_low, merge_full(n))
        )
        gain_grad_zero += gain_part
        part += sum_part
        wide_ref[n] = sum_part
        for m in range(count):
            sent_refs[m][n, 0] = wide_ref[n, :, lane_block(tm ^ m, width)].astype(bf16)
    part_ref[0] = part
    gain_grads_ref[0:1, :] += gain_grad_zero
    gain_grads_ref[1:2, :] += gain_grad_one
    gain_grads_ref[2:3, :] += gain_grad_two

    @pl.when(step == pl.num_programs(0) - 1)
    def finish():
        for m in range(count):
            t = tm ^ m
            lanes = lane_block(t, width)
            target, place = grad_refs[m], 0
            for e in range(tiles):
                value = grad_in_ref[t, :, e * width : (e + 1) * width]
                target[place : place + features, :] = value.astype(bf16)
                place += features
            for c in range(count):
                target[place : place + hidden, :] = grad_out_ref[c, :, lanes].astype(bf16)
                place += hidden
            for n in range(2):
                target[place : place + features, :] = grad_merge_ref[n, :, lanes].astype(bf16)
                place += features
            gain_rows = jnp.concatenate(
                [gain_grads_ref[:, lanes], jnp.zeros((8, width), f32)], axis=0
            )
            target[place : place + 16, :] = gain_rows.astype(bf16)


def rows_pass(sizes, tm, arrived, inputs, out_grad, back_rows, gains, weights, hidden, held):
    series, length, features = inputs.shape
    count, width = sizes.count, sizes.width
    rows = features * (hidden // width) + hidden * count + 2 * features + 16
    row_block = pl.BlockSpec((1, length, features), lambda s: (s, 0, 0))
    part_block = pl.BlockSpec((2, 1, length, width), lambda s: (0, s, 0, 0))
    per_row = 3 * (2 * features * features + 2 * features * hidden * count)
    outs = kernel_call(
        functools.partial(rows_body, sizes, hidden, len(held)),
        (series,),
        [SCALAR]
        + [part_block] * count
        + [row_block] * 3
        + [whole_block(gains.shape), whole_block(weights.shape)]
        + [pl.BlockSpec(memory_space=pl.ANY)] * len(held),
        [row_block, row_block] + [part_block] * count + [whole_block((rows, width))] * count,
        [jax.ShapeDtypeStruct(inputs.shape, bf16), jax.ShapeDtypeStruct(inputs.shape, f32)]
        + [jax.ShapeDtypeStruct(arrived[0].shape, bf16)] * count
        + [jax.ShapeDtypeStruct((rows, width), bf16)] * count,
        [
            pltpu.VMEM((count, length, hidden), f32),
            pltpu.VMEM((count, length, hidden), bf16),
            pltpu.VMEM((count, features, hidden), f32),
            pltpu.VMEM((count, hidden, features), f32),
            pltpu.VMEM((2, features, features), f32),
            pltpu.VMEM(gains.shape, f32),
            pltpu.VMEM((2, length, features), f32),
        ],
        2 * series * length * per_row,
        4 * count * rows * width + 24 * inputs.size,
    )(tm, *arrived, inputs, out_grad, back_rows, gains, weights, *held)
    return outs[0], outs[1], outs[2 : 2 + count], outs[2 + count :]


def stat_rows(packed_rows):
    return -(-packed_rows // 128) * 16


def up_back_body(sizes, steps, tm_ref, *refs):
    arrived_refs, refs = refs[: sizes.count], refs[sizes.count :]
    tanh_ref, sum_a_ref, sum_b_ref, gain_ref, up_a_ref, up_b_ref, grad_ref = refs[:7]
    sent_refs, refs = refs[7 : 7 + sizes.count], refs[7 + sizes.count :]
    low_ref, normed_a_ref, normed_b_ref, total_a_ref, total_b_ref = refs
    sum_refs = (sum_a_ref, sum_b_ref)
    normed_refs = (normed_a_ref, normed_b_ref)
    total_refs = (total_a_ref, total_b_ref)
    tm = tm_ref[0]
    step = pl.program_id(0)
    count, width, series = sizes.count, sizes.width, sizes.series

    @pl.when(step == 0)
    def start():
        for n in range(2):
            unit, unused = norm_parts(sum_refs[n][...])
            normed_refs[n][...] = (gain_ref[0:1, :] * unit).astype(bf16)
            total_refs[n][...] = jnp.zeros_like(total_refs[n])
            for s in range(series):
                for m in range(count):
                    place = pl.ds(pl.multiple_of((tm ^ m) * sizes.length, 16), sizes.length)
                    value = tanh_ref[n, s, place, :]
                    grad = arrived_refs[m][n, s].astype(f32) * (1.0 - value * value)
                    low_ref[n, s, place, :] = grad.astype(bf16).astype(f32)

    def taps(n, up_ref, first_tap):
        stride, rows, padded = sizes.strides[n], sizes.rows[n], sizes.padded[n]
        for pair in range(TAPS // 2):
            halves = []
            for half in range(2):
                place = pl.ds(first_tap + 2 * pair + half, rows, stride=stride)
                pieces = []
                for s in range(series):
                    pieces.append(low_ref[n, s, place, :])
                    if padded > rows:
                        pieces.append(jnp.zeros((padded - rows, width), f32))
                halves.append(jnp.concatenate(pieces, axis=0))
            low = jnp.concatenate(halves, axis=1).astype(bf16)
            both = jnp.concatenate([up_ref[2 * pair], up_ref[2 * pair + 1]], axis=1)
            total_refs[n][...] += matmul_nt(low, both)
            grad = matmul_tn(normed_refs[n][...], low).astype(bf16)
            grad_ref[2 * pair] = grad[:, :width]
            grad_ref[2 * pair + 1] = grad[:, width:]

    @pl.when(step < steps[0])
    def first_scale():
        taps(0, up_a_ref, step * TAPS)

    @pl.when(step >= steps[0])
    def second_scale():
        taps(1, up_b_ref, (step - steps[0]) * TAPS)

    @pl.when(step == pl.num_programs(0) - 1)
    def finish():
        columns = []
        for n in range(2):
            total = total_refs[n][...]
            padded = sizes.padded[n]
            unit, unused = norm_parts(sum_refs[n][...])
            lifted = gain_ref[0:1, :] * total
            columns.append(
                [
                    jnp.sum(lifted, axis=-1, keepdims=True),
                    jnp.sum(lifted * unit, axis=-1, keepdims=True),
                ]
            )
            for m in range(count):
                for s in range(series):
                    first = s * sizes.packed + sizes.starts[n]
                    sent_refs[m][first : first + padded, :] = total_refs[n][
                        s * padded : (s + 1) * padded, lane_block(tm ^ m, width)
                    ].astype(bf16)
        packed_rows = series * sizes.packed
        spread = -(-packed_rows // 128) * 128
        table = jnp.zeros((spread, 128), f32)
        lane = lax.broadcasted_iota(jnp.int32, (spread, 128), 1)
        for e in range(2):
            pieces = []
            for s in range(series):
                for n in range(2):
                    padded = sizes.padded[n]
                    pieces.append(columns[n][e][s * padded : (s + 1) * padded])
            if spread > packed_rows:
                pieces.append(jnp.zeros((spread - packed_rows, 1), f32))
            column = jnp.broadcast_to(jnp.concatenate(pieces, axis=0), (spread, 128))
            high = column.astype(bf16).astype(f32)
            table = jnp.where(lane == 2 * e, high, table)
            table = jnp.where(lane == 2 * e + 1, column - high, table)
        turned = table.T[:16, :].astype(bf16)
        for sent_ref in sent_refs:
            for e in range(spread // 128):
                first = packed_rows + 16 * e
                sent_ref[first : first + 16, :] = turned[:, e * 128 : (e + 1) * 128]


def up_backward(sizes, tm, arrived, up_tanh, sums, gains, up_a, up_b):
    steps, specs = tap_specs(sizes, (up_a, up_b))
    taps = up_a.shape[0] + up_b.shape[0]
    packed_rows = sizes.series * sizes.packed
    sent = (packed_rows + stat_rows(packed_rows), sizes.width)
    ready = (*arrived, up_tanh, *sums, gains)
    outs = kernel_call(
        functools.partial(up_back_body, sizes, steps),
        (sum(steps),),
        [SCALAR] + [whole_block(item.shape) for item in ready] + specs,
        [pl.BlockSpec((TAPS, sizes.features, sizes.width), lambda i: (i, 0, 0))]
        + [whole_block(sent)] * sizes.count,
        [jax.ShapeDtypeStruct((taps, sizes.features, sizes.width), bf16)]
        + [jax.ShapeDtypeStruct(sent, bf16)] * sizes.count,
        [pltpu.VMEM(up_tanh.shape, f32)]
        + [pltpu.VMEM(item.shape, bf16) for item in sums]
        + [pltpu.VMEM(item.shape, f32) for item in sums],
        8 * sizes.series * sizes.whole * sizes.features * sizes.width,
        4 * (up_a.size + up_b.size) + 12 * sizes.series * sizes.whole * sizes.width,
    )(tm, *ready, up_a, up_b)
    return outs[0], outs[1:]


def mix_back_body(sizes, lags, steps, tm_ref, *refs):
    arrived_refs, refs = refs[: sizes.count], refs[sizes.count :]
    sum_refs, coarse_own_ref, mixed_own_ref, iso_tanh_ref = refs[:2], *refs[2:5]
    gain_ref, iso_a_ref, iso_b_ref, upre_ref, iso_low_ref = refs[5:10]
    sent_refs, scratch = refs[10 : 10 + sizes.count], refs[10 + sizes.count :]
    low_refs, total_refs = scratch[:2], scratch[2:]
    tm = tm_ref[0]
    step = pl.program_id(0)
    width, series, features = sizes.width, sizes.series, sizes.features
    packed_rows = series * sizes.packed

    @pl.when(step == 0)
    def start():
        summed = arrived_refs[0][...].astype(f32)
        for ref in arrived_refs[1:]:
            summed += ref[...].astype(f32)
        tiles = -(-packed_rows // 128)
        turned = jnp.concatenate(
            [summed[packed_rows + 16 * m : packed_rows + 16 * (m + 1)] for m in range(tiles)],
            axis=1,
        )
        turned = jnp.concatenate([turned, jnp.zeros((112, 128 * tiles), f32)], axis=0)
        table = turned.T
        mean_lift = (table[:, 0:1] + table[:, 1:2]) / features
        mean_both = (table[:, 2:3] + table[:, 3:4]) / features
        gain_grad = jnp.zeros((1, width), f32)
        for n in range(2):
            padded = sizes.padded[n]
            field = sum_refs[n][...]
            mean = jnp.mean(field, axis=-1, keepdims=True)
            centred = field - mean
            spread = jnp.mean(centred * centred, axis=-1, keepdims=True)
            scale = lax.rsqrt(spread + epsilon)
            low_refs[n][...] = jnp.zeros_like(low_refs[n])
            total_refs[n][...] = jnp.zeros_like(total_refs[n])
            for s in range(series):
                local = slice(s * padded, (s + 1) * padded)
                place = slice(sizes.starts[n], sizes.starts[n] + padded)
                flat = slice(s * sizes.packed + place.start, s * sizes.packed + place.stop)
                own = coarse_own_ref[s, place, :].astype(f32)
                own += mixed_own_ref[s, place, :].astype(f32)
                unit = (own - mean[local]) * scale[local]
                upstream = summed[flat]
                grad = (
                    gain_ref[...] * upstream - mean_lift[flat] - unit * mean_both[flat]
                ) * scale[local]
                grad = jnp.where(row_mask(sizes, n, width), grad, 0.0)
                gain_grad += jnp.sum(upstream * unit, axis=0, keepdims=True)
                value = iso_tanh_ref[s, place, :]
                low = grad.astype(bf16).astype(f32) * (1.0 - value * value)
                low = low.astype(bf16)
                upre_ref[s, place, :] = grad
                iso_low_ref[flat, :] = low
                low_refs[n][s, 0:padded, :] = low.astype(f32)
        high = gain_grad.astype(bf16).astype(f32)
        gain_rows = jnp.concatenate(
            [high, gain_grad - high, jnp.zeros((14, width), f32)], axis=0
        )
        iso_low_ref[packed_rows:, :] = gain_rows.astype(bf16)

    def add_lags(n, kernel_ref, first_lag):
        padded = sizes.padded[n]
        kernel = jnp.concatenate([kernel_ref[e] for e in range(lags[n])], axis=1)
        sheared = jnp.concatenate(
            [
                jnp.concatenate(
                    [
                        low_refs[n][s, pl.ds(first_lag + e, padded), :].astype(bf16)
                        for e in range(lags[n])
                    ],
                    axis=1,
                )
                for s in range(series)
            ],
            axis=0,
        )
        total_refs[n][...] += matmul_nt(sheared, kernel)

    @pl.when(step < steps[0])
    def first_scale():
        add_lags(0, iso_a_ref, step * lags[0])

    @pl.when(step >= steps[0])
    def second_scale():
        add_lags(1, iso_b_ref, (step - steps[0]) * lags[1])

    @pl.when(step == pl.num_programs(0) - 1)
    def finish():
        for n in range(2):
            padded = sizes.padded[n]
            place = slice(sizes.starts[n], sizes.starts[n] + padded)
            for s in range(series):
                for m, sent_ref in enumerate(sent_refs):
                    sent_ref[s, place, :] = total_refs[n][
                        s * padded : (s + 1) * padded, lane_block(tm ^ m, width)
                    ].astype(bf16)


def mix_backward(
    sizes, tm, arrived, sums, coarse_own, mixed_own, iso_tanh, gain_own, iso_a, iso_b
):
    lags, steps, specs, flops = iso_steps(sizes)
    packed = (sizes.series, sizes.packed, sizes.width)
    low = (sizes.series * sizes.packed + 16, sizes.width)
    ready = (*arrived, *sums, coarse_own, mixed_own, iso_tanh, gain_own)
    outs = kernel_call(
        functools.partial(mix_back_body, sizes, lags, steps),
        (sum(steps),),
        [SCALAR] + [whole_block(item.shape) for item in ready] + specs,
        [whole_block(packed), whole_block(low)] + [whole_block(packed)] * sizes.count,
        [jax.ShapeDtypeStruct(packed, f32), jax.ShapeDtypeStruct(low, bf16)]
        + [jax.ShapeDtypeStruct(packed, bf16)] * sizes.count,
        [pltpu.VMEM((sizes.series, 2 * p, sizes.width), f32) for p in sizes.padded]
        + [pltpu.VMEM((sizes.series * p, sizes.features), f32) for p in sizes.padded],
        flops,
        2 * (iso_a.size + iso_b.size),
    )(tm, *ready, iso_a, iso_b)
    return outs[0], outs[1], outs[2:]


def down_back_body(sizes, tm_ref, *refs):
    arrived_refs, refs = refs[: sizes.count], refs[sizes.count :]
    upre_ref, tanh_ref, down_a_ref, down_b_ref, low_ref = refs[:5]
    sent_refs, steps_ref = refs[5 : 5 + sizes.count], refs[5 + sizes.count]
    head = 8
    value = tanh_ref[0]
    grad = upre_ref[0]
    for ref in arrived_refs:
        grad += ref[0].astype(f32)
    low = (grad * (1.0 - value * value)).astype(bf16)
    tiles, extent, lanes = steps_ref.shape
    last = head + sizes.whole - 16
    for c in range(tiles):
        steps_ref[c, last:, :] = jnp.zeros((extent - last, lanes), f32)
    for n, down_ref in enumerate((down_a_ref, down_b_ref)):
        stride, rows = sizes.strides[n], sizes.rows[n]
        part = low[sizes.starts[n] : sizes.starts[n] + sizes.padded[n]].astype(f32)
        part = jnp.where(row_mask(sizes, n, sizes.width), part, 0.0).astype(bf16)
        low_ref[0, sizes.starts[n] : sizes.starts[n] + sizes.padded[n], :] = part
        for r in range(stride):
            frame = matmul_nt(part, down_ref[r])[:rows]
            place = pl.ds(head - stride // 2 + r, rows, stride=stride)
            for c in range(tiles):
                piece = frame[:, c * lanes : (c + 1) * lanes]
                if n == 0:
                    steps_ref[c, place, :] = piece
                else:
                    steps_ref[c, place, :] += piece
    for m, sent_ref in enumerate(sent_refs):
        first = pl.multiple_of(head + (tm_ref[0] ^ m) * sizes.length, 8)
        for c in range(tiles):
            sent_ref[0, :, c * lanes : (c + 1) * lanes] = steps_ref[
                c, pl.ds(first, sizes.length), :
            ].astype(bf16)


def down_backward(sizes, tm, arrived, upre_grad, coarse_tanh, down_a, down_b):
    packed = (sizes.series, sizes.packed, sizes.width)
    block = pl.BlockSpec((1, sizes.packed, sizes.width), lambda s: (s, 0, 0))
    sent = (sizes.series, sizes.length, sizes.features)
    outs = kernel_call(
        functools.partial(down_back_body, sizes),
        (sizes.series,),
        [SCALAR]
        + [block] * (sizes.count + 2)
        + [whole_block(down_a.shape), whole_block(down_b.shape)],
        [block]
        + [pl.BlockSpec((1, sizes.length, sizes.features), lambda s: (s, 0, 0))] * sizes.count,
        [jax.ShapeDtypeStruct(packed, bf16)] + [jax.ShapeDtypeStruct(sent, bf16)] * sizes.count,
        [pltpu.VMEM((sizes.features // 128, 8 + sizes.whole + 16, 128), f32)],
        4 * sizes.series * sizes.whole * sizes.features * sizes.width,
        2 * (down_a.size + down_b.size) + 8 * sizes.series * sizes.whole * sizes.features,
    )(tm, *arrived, upre_grad, coarse_tanh, down_a, down_b)
    return outs[0], outs[1:]


def lag_grad_body(sizes, n, groups, group_ref, source_ref, spot_ref, *refs):
    piece_refs, (out_ref, moved_ref, grad_ref) = refs[:groups], refs[groups:]
    step = pl.program_id(0)
    part = source_ref.shape[0]
    first, padded, series = sizes.starts[n], sizes.padded[n], sizes.series

    @pl.when(step == 0)
    def start():
        source = source_ref[...].astype(f32)
        for p in range(SHIFTS):
            moved = pltpu.roll(source, p, axis=1) if p else source
            moved = jnp.where(spot_ref[0:1, :] >= p, moved, 0.0)
            moved_ref[p * part : (p + 1) * part, :] = moved.astype(bf16)
        grad_ref[...] = jnp.zeros_like(grad_ref)
        for k in range(groups):
            for s in range(series):
                place = s * sizes.packed + first
                grad_ref[(group_ref[0] ^ k) * series + s, 0:padded, :] = piece_refs[k][
                    place : place + padded, :
                ]

    halves = []
    for e in range(2):
        place = pl.ds(pl.multiple_of((2 * step + e) * SHIFTS, SHIFTS), padded)
        halves.append(
            jnp.concatenate([grad_ref[s, place, :] for s in range(groups * series)], axis=0)
        )
    total = matmul(moved_ref[...], jnp.concatenate(halves, axis=1))
    width = total.shape[1] // 2
    for e in range(2):
        for p in range(SHIFTS):
            out_ref[e * SHIFTS + p] = total[
                p * part : (p + 1) * part, e * width : (e + 1) * width
            ]


def lag_grad(sizes, n, group, source, pieces):
    part, columns = source.shape
    groups = len(pieces)
    lag_count, padded, width = sizes.rows[n], sizes.padded[n], sizes.width
    steps = -(-lag_count // (2 * SHIFTS))
    spot = jnp.broadcast_to(jnp.arange(columns, dtype=jnp.int32) % padded, (8, columns))
    return kernel_call(
        functools.partial(lag_grad_body, sizes, n, groups),
        (steps,),
        [SCALAR, whole_block(source.shape), whole_block(spot.shape)]
        + [whole_block(pieces[0].shape)] * groups,
        pl.BlockSpec((2 * SHIFTS, part, width), lambda i: (i, 0, 0)),
        jax.ShapeDtypeStruct((lag_count, part, width), f32),
        [
            pltpu.VMEM((SHIFTS * part, columns), bf16),
            pltpu.VMEM((groups * sizes.series, padded + 2 * SHIFTS * steps, width), bf16),
        ],
        2 * lag_count * part * width * columns,
        4 * lag_count * part * width,
    )(group, source, spot, *pieces)


def tap_grad_body(sizes, groups, group_ref, x_ref, *refs):
    low_refs, refs = refs[:groups], refs[groups:]
    out_refs, frames_refs, lows_refs, steps_ref = refs[:2], refs[2:4], refs[4:6], refs[6]
    width, series = sizes.width, sizes.series
    extra = x_ref.shape[1]
    steps_ref[extra:, :] = jnp.zeros((steps_ref.shape[0] - extra, 128), f32)
    halves = [m // 2 for m in sizes.rows]
    spans = [frames_refs[n].shape[0] // (groups * series) for n in range(2)]
    for n in range(2):
        half, span = halves[n], spans[n]
        for k in range(groups):
            for s in range(series):
                first = s * sizes.packed + sizes.starts[n]
                low = low_refs[k][first : first + sizes.padded[n], :].astype(f32)
                both = [low[:half], low[half : 2 * half]]
                pad = [jnp.zeros((span - half, width), f32)] if span > half else []
                both = jnp.concatenate(
                    [jnp.concatenate([item] + pad, axis=0) for item in both], axis=1
                )
                place = ((group_ref[0] ^ k) * series + s) * span
                lows_refs[n][pl.ds(pl.multiple_of(place, 8), span), :] = both
    for member in range(groups * series):
        steps_ref[0:extra, :] = x_ref[member].astype(f32)
        for n in range(2):
            stride, span = sizes.strides[n], spans[n]
            for r in range(stride):
                place = pl.ds(8 - stride // 2 + r, span, stride=stride)
                frames_refs[n][
                    member * span : (member + 1) * span, r * 128 : (r + 1) * 128
                ] = steps_ref[place, :]
    for n in range(2):
        lows = lows_refs[n][...].astype(bf16)
        for r in range(0, sizes.strides[n], 2):
            frames = frames_refs[n][:, r * 128 : (r + 2) * 128].astype(bf16)
            total = matmul_tn(frames, lows)
            for e in range(2):
                upper = total[e * 128 : e * 128 + 64, :width]
                lower = total[e * 128 + 64 : e * 128 + 128, width:]
                out_refs[n][r + e] = upper + lower


def tap_grad(sizes, group, x_parts, lows):
    groups, width = len(lows), sizes.width
    members, extra, unused = x_parts.shape
    spans = [-(-(m // 2) // 8) * 8 for m in sizes.rows]
    shapes = [(k, 64, width) for k in sizes.strides]
    extent = 8 + max(k * (m + 1) for k, m in zip(sizes.strides, spans))
    return kernel_call(
        functools.partial(tap_grad_body, sizes, groups),
        (),
        [SCALAR, whole_block(x_parts.shape)] + [whole_block(lows[0].shape)] * groups,
        [whole_block(shape) for shape in shapes],
        [jax.ShapeDtypeStruct(shape, f32) for shape in shapes],
        [
            pltpu.VMEM((members * span, k * 128), f32)
            for span, k in zip(spans, sizes.strides)
        ]
        + [pltpu.VMEM((members * span, 2 * width), f32) for span in spans]
        + [pltpu.VMEM((extent, 128), f32)],
        8 * members * sizes.whole * 64 * width,
        2 * x_parts.size + 8 * sum(sizes.strides) * 64 * width,
    )(group, x_parts, *lows)


def lag_grad_plain(lag_count, padded, source, grad):
    part = source.shape[0]
    series, unused, width = grad.shape
    blocks = -(-lag_count // SHIFTS)
    source = source.reshape(part, series, padded).transpose(2, 1, 0)
    source = jnp.pad(source, ((SHIFTS, 0), (0, 0), (0, 0)))
    stacked = jnp.stack(
        [source[SHIFTS - p : SHIFTS - p + padded] for p in range(SHIFTS)], axis=2
    )
    stacked = stacked.reshape(padded * series, SHIFTS * part)
    target = jnp.pad(grad.transpose(1, 0, 2), ((0, blocks * SHIFTS), (0, 0), (0, 0)))
    moved = jnp.stack(
        [target[q * SHIFTS : q * SHIFTS + padded] for q in range(blocks)], axis=2
    )
    moved = moved.reshape(padded * series, blocks * width)
    total = dot32("ra,rb->ab", stacked, moved).reshape(SHIFTS, part, blocks, width)
    return total.transpose(2, 0, 1, 3).reshape(blocks * SHIFTS, part, width)[:lag_count]


def swapped(block, axis, mask):
    route = [(i, i ^ mask) for i in range(lax.axis_size(axis))]
    return lax.ppermute(block, axis, route)


def gather_pieces(block, axis):
    return [block] + [swapped(block, axis, m) for m in range(1, lax.axis_size(axis))]


def gather_by_chip(block):
    across = swapped(block, "tm", 2)
    return [block, swapped(block, "tm", 1), across, swapped(across, "tm", 1)]


def exchange(pieces):
    return [pieces[0]] + [swapped(pieces[m], "tm", m) for m in range(1, len(pieces))]


def reduce_by_chip(pieces):
    near = swapped(pieces[1], "tm", 1)
    far = swapped(pieces[3], "tm", 1)
    across = (pieces[2].astype(f32) + far.astype(f32)).astype(bf16)
    across = swapped(across, "tm", 2)
    return pieces[0].astype(f32) + near.astype(f32) + across.astype(f32)


def in_order(pieces, tm):
    odd, late = (tm & 1) == 1, (tm & 2) == 2
    first = [jnp.where(odd, pieces[m ^ 1], pieces[m]) for m in range(4)]
    return [jnp.where(late, first[m ^ 2], first[m]) for m in range(4)]


def weight_rows(merge, ffn_in, ffn_out, width):
    tiles = ffn_in.shape[1] // width
    columns = [ffn_in[:, e * width : (e + 1) * width] for e in range(tiles)]
    return columns, ffn_out, merge.reshape(-1, width)


def gather_weights(merge, ffn_in, ffn_out, width, group, groups):
    columns, out_rows, merge_rows = weight_rows(merge, ffn_in, ffn_out, width)
    if groups != 8:
        own = jnp.concatenate([*columns, out_rows, merge_rows], axis=0)
        return lax.all_gather(own, "tm", axis=0, tiled=False)[None]

    def chunk(rows):
        held = rows.shape[0] // groups
        return lax.dynamic_slice_in_dim(rows, group * held, held, axis=0)

    own = jnp.concatenate([chunk(item) for item in (*columns, out_rows, merge_rows)], axis=0)
    whole = lax.all_gather(own, ("series", "tm"), axis=0, tiled=False)
    return whole.reshape(groups, -1, *own.shape)


def shards(
    inputs,
    cotangent,
    horizon,
    down_a,
    down_b,
    up_a,
    up_b,
    iso_a,
    iso_b,
    merge,
    ffn_in,
    ffn_out,
    gain0,
    gain1,
    gain2,
    regress,
):
    series, length, features = inputs.shape
    tm = lax.axis_index("tm")
    group = lax.axis_index("series")
    count = lax.axis_size("tm")
    groups = lax.axis_size("series")
    sizes = Sizes(series, length, features, count, (down_a.shape[0], down_b.shape[0]))
    width, whole, packed = sizes.width, sizes.whole, sizes.packed
    part = features // groups
    hidden = ffn_in.shape[1]
    tm_word = tm.astype(jnp.int32).reshape(1)
    group_word = group.astype(jnp.int32).reshape(1)
    direct = groups == 8 and part == 64

    x_pieces = gather_by_chip(inputs)
    gains = lax.all_gather(jnp.stack([gain0, gain1, gain2]), "tm", axis=1, tiled=True)
    gains = jnp.pad(gains.astype(f32), ((0, 5), (0, 0)))
    weights = gather_weights(merge, ffn_in, ffn_out, width, group, groups)

    positions = tm * length + jnp.arange(length, dtype=jnp.int32)
    valid_len = LEN - (720 - horizon) * LEN // 960
    loss_mask = (positions[None, :] < valid_len[:, None]).astype(f32)
    out_grad = (cotangent.astype(f32) * loss_mask[:, :, None]).astype(bf16)
    columns = in_order([regress[:, t * length : (t + 1) * length] for t in range(count)], tm)
    back_rows = reduce_by_chip(
        [dot32("tu,std->sud", column, out_grad).astype(bf16) for column in columns]
    ).astype(bf16)

    coarse_tanh, coarse_own, x_sent = down_forward(
        sizes, groups, tm_word, x_pieces, down_a, down_b
    )
    coarse_pieces = gather_pieces(coarse_own, "tm")
    iso_tanh, mixed_own = iso_forward(sizes, tm_word, coarse_pieces, iso_a, iso_b)
    mixed_pieces = gather_pieces(mixed_own, "tm")
    up_tanh, up_sent, sums = up_forward(
        sizes, tm_word, coarse_pieces, mixed_pieces, gains, up_a, up_b
    )
    coarse_full = jnp.concatenate(in_order(coarse_pieces, tm), axis=2)
    coarse_part = lax.all_to_all(
        coarse_full, "series", split_axis=2, concat_axis=0, tiled=True
    )
    sources = [
        coarse_part[:, first : first + padded].transpose(2, 0, 1).reshape(part, -1)
        for first, padded in zip(sizes.starts, sizes.padded)
    ]
    held = []
    if direct:
        x_parts = lax.all_to_all(x_sent, "series", split_axis=0, concat_axis=0, tiled=True)
        x_parts = x_parts.reshape(groups * series, *x_sent.shape[2:])
        held = [x_parts, *sources]
    season, input_part, back_sent, weight_parts = rows_pass(
        sizes,
        tm_word,
        exchange(up_sent),
        inputs,
        out_grad,
        back_rows,
        gains,
        weights,
        hidden,
        held,
    )
    back_arrived = exchange(back_sent)
    seasons = gather_by_chip(season)
    trend = sum(
        dot32("tu,sud->std", column, item) for column, item in zip(columns, seasons)
    )
    output = (season.astype(f32) + trend).astype(bf16)
    regress_parts = [dot32("std,sud->tu", out_grad, item).astype(bf16) for item in seasons]
    weight_sums = reduce_by_chip(weight_parts).astype(bf16)
    weight_sums, regress_sums = lax.psum(
        (weight_sums, jnp.concatenate(regress_parts, axis=0)), "series"
    )

    grad_ups, normed_sent = up_backward(
        sizes, tm_word, back_arrived, up_tanh, sums, gains, up_a, up_b
    )
    grad_ups = lax.psum_scatter(grad_ups, "series", scatter_dimension=1, tiled=True)
    gain_own = lax.dynamic_slice_in_dim(gains[0:1], tm * width, width, axis=1)
    upre_grad, iso_low, coarse_sent = mix_backward(
        sizes,
        tm_word,
        exchange(normed_sent),
        sums,
        coarse_own,
        mixed_own,
        iso_tanh,
        gain_own,
        iso_a,
        iso_b,
    )
    down_low, frames_sent = down_backward(
        sizes, tm_word, exchange(coarse_sent), upre_grad, coarse_tanh, down_a, down_b
    )
    input_grad = (input_part + reduce_by_chip(frames_sent)).astype(bf16)

    packed_rows = series * packed
    if direct:
        iso_lows = gather_pieces(iso_low, "series")
        down_lows = gather_pieces(down_low.reshape(packed_rows, width), "series")
        gain_part = sum(
            jnp.sum(item[packed_rows : packed_rows + 2].astype(f32), axis=0)
            for item in iso_lows
        )
        grad_isos = [lag_grad(sizes, n, group_word, sources[n], iso_lows) for n in range(2)]
        grad_downs = tap_grad(sizes, group_word, x_parts, down_lows)
    else:
        iso_all = lax.all_gather(iso_low, "series", axis=0, tiled=False)
        down_all = lax.all_gather(down_low, "series", axis=0, tiled=True)
        gain_part = jnp.sum(iso_all[:, packed_rows : packed_rows + 2].astype(f32), axis=(0, 1))
        iso_all = iso_all[:, :packed_rows].reshape(groups * series, packed, width)
        x_full = jnp.concatenate(in_order(x_pieces, tm), axis=1)
        x_parts = lax.all_to_all(x_full, "series", split_axis=2, concat_axis=0, tiled=True)
        grad_downs, grad_isos = [], []
        for n in range(2):
            stride, rows, padded = sizes.strides[n], sizes.rows[n], sizes.padded[n]
            place = slice(sizes.starts[n], sizes.starts[n] + padded)
            frames = jnp.pad(x_parts, ((0, 0), (stride // 2, 0), (0, 0)))[:, :whole]
            frames = frames.reshape(series * groups, rows, stride, part)
            frames = jnp.pad(frames, ((0, 0), (0, padded - rows), (0, 0), (0, 0)))
            frames = frames.transpose(2, 3, 0, 1).reshape(stride * part, -1)
            low = down_all[:, place].reshape(-1, width)
            grad_downs.append(dot32("ar,ro->ao", frames, low).reshape(stride, part, width))
            grad_isos.append(lag_grad_plain(rows, padded, sources[n], iso_all[:, place]))

    first = features * (hidden // width)
    second = first + hidden * count
    third = second + 2 * features
    grad_in = jnp.concatenate(
        [weight_sums[e * features : (e + 1) * features] for e in range(hidden // width)], axis=1
    )
    grad_out = weight_sums[first:second]
    grad_merge = weight_sums[second:third].reshape(2, features, width)
    gain_grads = weight_sums[third : third + 3].astype(f32)
    grad_regress = [regress_sums[t * length : (t + 1) * length] for t in range(count)]
    grad_regress = jnp.concatenate(in_order(grad_regress, tm), axis=1)
    taps = down_a.shape[0]
    return (
        output,
        input_grad,
        grad_downs[0],
        grad_downs[1],
        grad_ups[:taps].astype(f32),
        grad_ups[taps:].astype(f32),
        grad_isos[0],
        grad_isos[1],
        grad_merge.astype(f32),
        grad_in.astype(f32),
        grad_out.astype(f32),
        gain_grads[0] + gain_part,
        gain_grads[1],
        gain_grads[2],
        grad_regress.astype(f32),
    )


def solution(mesh):
    return jax.shard_map(
        shards,
        mesh=mesh,
        in_specs=(
            P("series", "tm", None),
            P("series", "tm", None),
            P("series"),
            P(None, None, "tm"),
            P(None, None, "tm"),
            P(None, None, "tm"),
            P(None, None, "tm"),
            P(None, None, "tm"),
            P(None, None, "tm"),
            P(None, None, "tm"),
            P(None, "tm"),
            P(None, "tm"),
            P("tm"),
            P("tm"),
            P("tm"),
            P("tm", None),
        ),
        out_specs=(
            P("series", "tm", None),
            P("series", "tm", None),
            P(None, "series", "tm"),
            P(None, "series", "tm"),
            P(None, "series", "tm"),
            P(None, "series", "tm"),
            P(None, "series", "tm"),
            P(None, "series", "tm"),
            P(None, None, "tm"),
            P(None, "tm"),
            P(None, "tm"),
            P("tm"),
            P("tm"),
            P("tm"),
            P("tm", None),
        ),
        check_vma=False,
    )
```

time: 888 us -> 568 us (0.64)
  local copies, waits for them, and re-layouts: 288 us -> 23.8 us
  Pallas kernels: 31.5 us -> 162 us
  matrix products: 134 us -> 14.9 us
  other arithmetic: 82.9 us -> 36.7 us
  blocking collectives: 84 us -> 45.5 us
  starting transfers between devices: 32.8 us -> 52.9 us
    ppermute x0 -> x47, waiting for transfers between devices: none -> 199 us  [swapped(): return lax.ppermute(block, axis, route)]
    pallas_call x4 -> x10, Pallas kernels: 31.5 us -> 162 us  [the longest x1 45.1 us: rows_pass(): kernel_call(functools.partial(rows_body, sizes, hidden, len(held)), (seri...]
    dot_general x27 -> x12, matrix products: 113 us -> 14.9 us  [dot32(): return jnp.einsum(spec, a, b, preferred_element_type=f32)]
    psum x1, waiting for transfers between devices: 70.9 us -> 0.01 us  [shards(): lax.psum((weight_sums, jnp.concatenate(regress_parts, axis=0)), 'series')]
    unnamed x204 -> x102, local copies, waits for them, and re-layouts: 78.7 us -> 9.06 us
    all_to_all x7 -> x1, waiting for transfers between devices: 73.5 us -> 12.4 us  [shards(): lax.all_to_all(x_sent, 'series', split_axis=0, concat_axis=0, tiled=True)]
    ppermute x0 -> x47, starting transfers between devices: none -> 48.1 us  [swapped(): return lax.ppermute(block, axis, route)]
    reshape x8 -> x2, local copies, waits for them, and re-layouts: 43.7 us -> 2.05 us  [shards(): coarse_part[:, first:first + padded].transpose(2, 0, 1).reshape(part, -1)]
  transfers between devices with their start and end apart: 22 -> 51, of which waited for: 9 -> 23; matrix products, arithmetic and copies ran while one was open for 51% -> 11% of each run, Pallas kernels for 4% -> 21%
where the time goes in v2:
time: 568 us; the launch traced here: 562 us
  waiting for transfers between devices  212 us (37%)
  Pallas kernels  162 us (29%)
  starting transfers between devices  52.9 us (9%)
  blocking collectives  45.5 us (8%)
  other arithmetic  36.7 us (6%)
  local copies, waits for them, and re-layouts  23.8 us (4%)
  matrix products  14.9 us (3%)
  between operations  14.6 us (3%)
    ppermute x47, waiting for transfers between devices, swapped(): return lax.ppermute(block, axis, route)  199 us
    ppermute x47, starting transfers between devices, swapped(): return lax.ppermute(block, axis, route)  48.1 us
    pallas_call x1, Pallas kernels, rows_pass(): kernel_call(functools.partial(rows_body, sizes, hidden, len(held)), (seri...  45.1 us
    all_to_all x1, blocking collectives, shards(): lax.all_to_all(coarse_full, 'series', split_axis=2, concat_axis=0, tiled=...  39.9 us
    pallas_call x1, Pallas kernels, mix_backward(): kernel_call(functools.partial(mix_back_body, sizes, lags, steps), (sum(st...  21.2 us
    pallas_call x1, Pallas kernels, iso_forward(): kernel_call(functools.partial(iso_body, sizes, lags, steps), (sum(steps),...  20.1 us
    pallas_call x2, Pallas kernels, lag_grad(): kernel_call(functools.partial(lag_grad_body, sizes, n, groups), (steps,),...  18.9 us
    dot_general x12, matrix products, dot32(): return jnp.einsum(spec, a, b, preferred_element_type=f32)  14.9 us
  transfers between devices with their start and end apart: 51, of which 23 were waited for; matrix products, arithmetic and copies ran while one was open for 11% of the time, Pallas kernels for 21%

profile of v2, /device:TPU:0, one launch (start us, length us, event | category | flops | bytes accessed | tf_op | source)
XLA Modules:
  0.0 561.7 jit_solution(14468723632516284646)
XLA Ops:
  13.9 20.6 %collective-permute-done.1.refs_2_ = bf16[3,336,512]{2,1,0:T(8,128)(2,1)S(1)} collective-permute-done((bf16[3,336,512]{2,1,0:T(8,128)(2,1)}, bf16[3,336,512]{2,1,0:T(8,128)(2,1)S(1)}, u32[]{:S(2)}, u32[]{:S(2)}) %collective-permute-start.1) | collective-permute-done | bytes 1032224 | tf_op jit(solution)/shard_map/ppermute | solution.py:980
  38.0 9.4 %shard_map.271 = (f32[3,208,128]{2,1,0:T(8,128)}, bf16[3,208,128]{2,1,0:T(8,128)(2,1)}, bf16[8,3,680,128]{3,2,1,0:T(8,128)(2,1)}) custom-call(s32[1]{0:T(128)} %bitcast.tm_ref, bf16[3,336,512]{2,1,0:T(8,128)(2,1)} %refs_4_.5, bf16[3,336,512]{2,1,0:T(8,128)(2,1)} %copy-done.9, bf16[3,336,512]{2,1,0:T(8,128)(2,1)} %copy-done.8, ...), custom_call_target="tpu_custom_call" | custom-call | flops 1056964608 | bytes 11927552 | tf_op jit(solution)/shard_map/pallas_call | solution.py:172
  49.3 4.4 collective-permute-done.5.refs_3_
  59.4 39.9 %all_to_all.23 = bf16[3,208,512]{1,0,2:T(4,128)(2,1)} all-to-all(bf16[3,208,512]{1,0,2:T(4,128)(2,1)S(1)} %copy.58), channel_id=1, replica_groups=mesh['series'=8,'tm'=4] {'series'}, dimensions={2} | all-to-all | bytes 1277952 | tf_op jit(solution)/shard_map/all_to_all | solution.py:1086
  99.3 4.7 all-to-all-start
  108.9 5.5 all_gather.9
  118.2 20.1 %shard_map.272 = (f32[3,208,128]{2,1,0:T(8,128)}, bf16[3,208,128]{2,1,0:T(8,128)(2,1)}) custom-call(s32[1]{0:T(128)} %bitcast.tm_ref, bf16[3,208,128]{2,1,0:T(8,128)(2,1)} %get-tuple-element.55.refs_0_.refs_6_, bf16[3,208,128]{2,1,0:T(8,128)(2,1)} %copy-done.20, bf16[3,208,128]{2,1,0:T(8,128)(2,1)} %copy-done.19, bf16[3,208,128]{2,1,0:T(8,128)(2,1)} %copy-done.18, ...), custom_call_target="tpu_custom_call" | custom-call | flops 8103395328 | bytes 25690112 | tf_op jit(solution)/shard_map/pallas_call | solution.py:259
  140.9 4.2 collective-permute-done.8.refs_7_
  145.1 3.8 collective-permute-done.7.refs_6_
  149.0 10.2 %shard_map.273 = (f32[2,3,1344,128]{3,2,1,0:T(8,128)}, bf16[2,3,336,128]{3,2,1,0:T(8,128)(2,1)}, bf16[2,3,336,128]{3,2,1,0:T(8,128)(2,1)}, bf16[2,3,336,128]{3,2...) custom-call(s32[1]{0:T(128)} %bitcast.tm_ref, ...), custom_call_target="tpu_custom_call" | custom-call | flops 1056964608 | bytes 9863168 | tf_op jit(solution)/shard_map/pallas_call | solution.py:347
  166.7 7.4 %collective-permute-done.10.refs_2_ = bf16[2,3,336,128]{3,2,1,0:T(8,128)(2,1)} collective-permute-done((bf16[2,3,336,128]{3,2,1,0:T(8,128)(2,1)}, bf16[2,3,336,128]{3,2,1,0:T(8,128)(2,1)}, u32[]{:S(2)}, u32[]{:S(2)}) %collective-permute-start.10) | collective-permute-done | bytes 516128 | tf_op jit(solution)/shard_map/ppermute | solution.py:980
  174.1 10.1 %collective-permute-done.11.refs_3_ = bf16[2,3,336,128]{3,2,1,0:T(8,128)(2,1)} collective-permute-done((bf16[2,3,336,128]{3,2,1,0:T(8,128)(2,1)}, bf16[2,3,336,128]{3,2,1,0:T(8,128)(2,1)}, u32[]{:S(2)}, u32[]{:S(2)}) %collective-permute-start.11) | collective-permute-done | bytes 516128 | tf_op jit(solution)/shard_map/ppermute | solution.py:980
  184.2 12.4 %all-to-all-done = bf16[8,3,680,128]{3,2,1,0:T(8,128)(2,1)} async-done(((bf16[8,3,680,128]{3,2,1,0:T(8,128)(2,1)}), bf16[8,3,680,128]{3,2,1,0:T(8,128)(2,1)}, u32[]{:S(2)}, u32[]{:S(2)}) %all-to-all-start) | async-done | bytes 4177952 | tf_op jit(solution)/shard_map/all_to_all | solution.py:1095
  196.6 45.1 %shard_map.274 = (bf16[3,336,512]{2,1,0:T(8,128)(2,1)}, f32[3,336,512]{2,1,0:T(8,128)}, bf16[2,3,336,128]{3,2,1,0:T(8,128)(2,1)}, bf16[2,3,336,128]{3,2,1,0:T(8,...) custom-call(s32[1]{0:T(128)} %bitcast.tm_ref, ...), custom_call_target="tpu_custom_call" | custom-call | flops 15854469120 | bytes 22904832 | tf_op jit(solution)/shard_map/pallas_call | solution.py:512
  243.9 23.4 %collective-permute-done.16 = bf16[3,336,512]{2,1,0:T(8,128)(2,1)S(1)} collective-permute-done((bf16[3,336,512]{2,1,0:T(8,128)(2,1)}, bf16[3,336,512]{2,1,0:T(8,128)(2,1)S(1)}, u32[]{:S(2)}, u32[]{:S(2)}) %collective-permute-start.16) | collective-permute-done | bytes 1032224 | tf_op jit(solution)/shard_map/ppermute | solution.py:980
  281.0 20.6 %collective-permute-done.46 = bf16[5136,128]{1,0:T(8,128)(2,1)} collective-permute-done((bf16[5136,128]{1,0:T(8,128)(2,1)}, bf16[5136,128]{1,0:T(8,128)(2,1)}, u32[]{:S(2)}, u32[]{:S(2)}) %collective-permute-start.46) | collective-permute-done | bytes 1314848 | tf_op jit(solution)/shard_map/ppermute | solution.py:980
  307.2 12.7 %collective-permute-done.19.refs_2_ = bf16[2,3,336,128]{3,2,1,0:T(8,128)(2,1)S(1)} collective-permute-done((bf16[2,3,336,128]{3,2,1,0:T(8,128)(2,1)}, bf16[2,3,336,128]{3,2,1,0:T(8,128)(2,1)S(1)}, u32[]{:S(2)}, u32[]{:S(2)}) %collective-permute-start.19) | collective-permute-done | bytes 516128 | tf_op jit(solution)/shard_map/ppermute | solution.py:980
  319.9 10.2 %collective-permute-done.20.refs_3_ = bf16[2,3,336,128]{3,2,1,0:T(8,128)(2,1)S(1)} collective-permute-done((bf16[2,3,336,128]{3,2,1,0:T(8,128)(2,1)S(1)}, bf16[2,3,336,128]{3,2,1,0:T(8,128)(2,1)S(1)}, u32[]{:S(2)}, u32[]{:S(2)}) %collective-permute-start.20) | collective-permute-done | bytes 516128 | tf_op jit(solution)/shard_map/ppermute | solution.py:980
  330.8 13.6 %shard_map.275 = (bf16[28,512,128]{2,1,0:T(8,128)(2,1)}, bf16[704,128]{1,0:T(8,128)(2,1)}, bf16[704,128]{1,0:T(8,128)(2,1)}, bf16[704,128]{1,0:T(8,128)(2,1)}, bf16[704,128]{1,0:T(8,128)(2,1)}) custom-call(s32[1]{0:T(128)} %bitcast.tm_ref, bf16[2,3,336,128]{3,2,1,0:T(8,128)(2,1)} %get-tuple-element.64.refs_0_, bf16[2,3,336,128]{3,2,1,0:T(8,128)(2,1)} %copy-done.21, ...), custom_call_target="tpu_custom_call" | custom-call | flops 2113929216 | bytes 13533184 | tf_op jit(solution)/shard_map/pallas_call | solution.py:644
  349.0 4.8 collective-permute-done.22.refs_2_
  356.6 21.2 %shard_map.276 = (f32[3,208,128]{2,1,0:T(8,128)}, bf16[640,128]{1,0:T(8,128)(2,1)}, bf16[3,208,128]{2,1,0:T(8,128)(2,1)}, bf16[3,208,128]{2,1,0:T(8,128)(2,1)}, ...) custom-call(s32[1]{0:T(128)} %bitcast.tm_ref, bf16[704,128]{1,0:T(8,128)(2,1)} %get-tuple-element.71.refs_0_, ...), custom_call_target="tpu_custom_call" | custom-call | flops 8103395328 | bytes 25690112 | tf_op jit(solution)/shard_map/pallas_call | solution.py:766
  389.9 11.4 %shard_map.277 = (bf16[3,208,128]{2,1,0:T(8,128)(2,1)}, bf16[3,336,512]{2,1,0:T(8,128)(2,1)}, bf16[3,336,512]{2,1,0:T(8,128)(2,1)}, bf16[3,336,512]{2,1,0:T(8,128)(2,1)}, bf16[3,336,512]{2,1,0:T(8,128)(2,1)}) custom-call(s32[1]{0:T(128)} %bitcast.tm_ref, bf16[3,208,128]{2,1,0:T(8,128)(2,1)} %get-tuple-element.76.refs_0_, ...), custom_call_target="tpu_custom_call" | custom-call | flops 1056964608 | bytes 20185088 | tf_op jit(solution)/shard_map/pallas_call | solution.py:821
  407.3 20.6 %collective-permute-done.41.refs_5_ = bf16[640,128]{1,0:T(8,128)(2,1)} collective-permute-done((bf16[640,128]{1,0:T(8,128)(2,1)}, bf16[640,128]{1,0:T(8,128)(2,1)}, u32[]{:S(2)}, u32[]{:S(2)}) %collective-permute-start.41) | collective-permute-done | bytes 163872 | tf_op jit(solution)/shard_map/ppermute | solution.py:980
  427.9 6.1 %collective-permute-start.36 = (bf16[624,128]{1,0:T(8,128)(2,1)}, bf16[624,128]{1,0:T(8,128)(2,1)}, u32[]{:S(2)}, u32[]{:S(2)}) collective-permute-start(bf16[624,128]{1,0:T(8,128)(2,1)} %bitcast.108), channel_id=1, source_target_pairs={{0,28},{4,24},{8,20},{12,16},{16,12},{20,8},{24,4},{28,0},{1,29},{... | collective-permute-start | bytes 479240 | tf_op jit(solution)/shard_map/ppermute | solution.py:980
  435.1 4.7 collective-permute-done.40.refs_4_
  446.5 8.0 %shard_map.280 = f32[84,64,128]{2,1,0:T(8,128)} custom-call(s32[1]{0:T(128)} %bitcast.25.group_ref, bf16[64,2304]{1,0:T(8,128)(2,1)} %reshape.95.refs_11_.source_ref, s32[8,2304]{1,0:T(8,128)} %broadcast_in_dim.10.spot_ref, bf16[640,128]{1,0:T(8,128)(2,1)} %get-tuple-element.90.refs_0_, bf16[640,128]{1,0:T(8,128)(2,1)} %collective-permute-done.37.refs_1_, ...), custom_call_target="tpu_custom_call" | custom-call | flops 3170893824 | bytes 2752512 | tf_op jit(solution)/shard_map/pallas_call | solution.py:879
  455.8 10.9 %shard_map.279 = f32[112,64,128]{2,1,0:T(8,128)} custom-call(s32[1]{0:T(128)} %bitcast.25.group_ref, bf16[64,2688]{1,0:T(8,128)(2,1)} %reshape.94.refs_10_.source_ref, s32[8,2688]{1,0:T(8,128)} %broadcast_in_dim.4.spot_ref, bf16[640,128]{1,0:T(8,128)(2,1)} %get-tuple-element.90.refs_0_, bf16[640,128]{1,0:T(8,128)(2,1)} %collective-permute-done.37.refs_1_, ...), custom_call_target="tpu_custom_call" | custom-call | flops 4932501504 | bytes 3670016 | tf_op jit(solution)/shard_map/pallas_call | solution.py:879
  477.3 4.7 collective-permute-done.33.refs_4_
  482.0 8.9 %collective-permute-done.32.refs_3_ = bf16[624,128]{1,0:T(8,128)(2,1)} collective-permute-done((bf16[624,128]{1,0:T(8,128)(2,1)}, bf16[624,128]{1,0:T(8,128)(2,1)}, u32[]{:S(2)}, u32[]{:S(2)}) %collective-permute-start.32) | collective-permute-done | bytes 159776 | tf_op jit(solution)/shard_map/ppermute | solution.py:980
  490.9 7.8 %collective-permute-done.31.refs_2_ = bf16[624,128]{1,0:T(8,128)(2,1)} collective-permute-done((bf16[624,128]{1,0:T(8,128)(2,1)}, bf16[624,128]{1,0:T(8,128)(2,1)}, u32[]{:S(2)}, u32[]{:S(2)}) %collective-permute-start.31) | collective-permute-done | bytes 159776 | tf_op jit(solution)/shard_map/ppermute | solution.py:980
  498.6 11.8 %shard_map.278 = (f32[12,64,128]{2,1,0:T(8,128)}, f32[16,64,128]{2,1,0:T(8,128)}) custom-call(s32[1]{0:T(128)} %bitcast.25.group_ref, bf16[24,680,128]{2,1,0:T(8,128)(2,1)} %bitcast.14.refs_9_.x_ref, bf16[624,128]{1,0:T(8,128)(2,1)} %bitcast.115, bf16[624,128]{1,0:T(8,128)(2,1)} %collective-permute-done.30.refs_1_, ...), custom_call_target="tpu_custom_call" | custom-call | flops 2113929216 | bytes 6012928 | tf_op jit(solution)/shard_map/pallas_call | solution.py:942
  518.0 19.1 %collective-permute-done.29 = bf16[3,336,512]{2,1,0:T(8,128)(2,1)S(1)} collective-permute-done((bf16[3,336,512]{2,1,0:T(8,128)(2,1)S(1)}, bf16[3,336,512]{2,1,0:T(8,128)(2,1)S(1)}, u32[]{:S(2)}, u32[]{:S(2)}) %collective-permute-start.29) | collective-permute-done | bytes 1032224 | tf_op jit(solution)/shard_map/ppermute | solution.py:980
  (252 shorter events, 128.8 us)
Async XLA Ops:
  7.2 189.5 %all-gather.3.cloned.1.call-start = ((), (), s32[]{:S(2)}) async-start(), calls=%async_computation.4 | async-start | bytes 5406720 | tf_op jit(solution)/shard_map/all_gather | solution.py:1027
  7.2 27.2 %collective-permute-start.1 = (bf16[3,336,512]{2,1,0:T(8,128)(2,1)}, bf16[3,336,512]{2,1,0:T(8,128)(2,1)S(1)}, u32[]{:S(2)}, u32[]{:S(2)}) collective-permute-start(bf16[3,336,512]{2,1,0:T(8,128)(2,1)} %refs_4_.5), channel_id=1, source_target_pairs={{0,2},{1,3},{2,0},{3,1},{4,6},{5,7},{6,4},{7,5},{8,10},{9,11},{10,... | collective-permute-start | bytes 3096584 | tf_op jit(solution)/shard_map/ppermute | solution.py:980
  13.8 20.6 %collective-permute-start = (bf16[3,336,512]{2,1,0:T(8,128)(2,1)}, bf16[3,336,512]{2,1,0:T(8,128)(2,1)S(1)}, u32[]{:S(2)}, u32[]{:S(2)}) collective-permute-start(bf16[3,336,512]{2,1,0:T(8,128)(2,1)} %refs_4_.5), channel_id=1, source_target_pairs={{0,1},{1,0},{2,3},{3,2},{4,5},{5,4},{6,7},{7,6},{8,9},{9,8},{10,11... | collective-permute-start | bytes 3096584 | tf_op jit(solution)/shard_map/ppermute | solution.py:980
  99.3 97.3 %all-to-all-start = ((bf16[8,3,680,128]{3,2,1,0:T(8,128)(2,1)}), bf16[8,3,680,128]{3,2,1,0:T(8,128)(2,1)}, u32[]{:S(2)}, u32[]{:S(2)}) async-start(bf16[8,3,680,128]{3,2,1,0:T(8,128)(2,1)} %get-tuple-element.61), calls=%async_computation | async-start | bytes 8355840 | tf_op jit(solution)/shard_map/all_to_all | solution.py:1095
  104.0 435.9 %all-reduce.4.cloned.1.call-start = ((), (), s32[]{:S(2)}) async-start(), calls=%async_computation.5 | async-start | bytes 4521984 | tf_op jit(solution)/shard_map/psum | solution.py:1118
  108.4 52.6 %collective-permute-start.12 = (bf16[3,336,512]{2,1,0:T(8,128)(2,1)}, bf16[3,336,512]{2,1,0:T(8,128)(2,1)S(1)}, u32[]{:S(2)}, u32[]{:S(2)}) collective-permute-start(bf16[3,336,512]{2,1,0:T(8,128)(2,1)} %fusion.4), channel_id=1, source_target_pairs={{0,1},{1,0},{2,3},{3,2},{4,5},{5,4},{6,7},{7,6},{8,9},{9,8},{10,11... | collective-permute-start | bytes 3096584 | tf_op jit(solution)/shard_map/ppermute | solution.py:980
  116.8 44.3 %collective-permute-start.14 = (bf16[3,336,512]{2,1,0:T(8,128)(2,1)}, bf16[3,336,512]{2,1,0:T(8,128)(2,1)}, u32[]{:S(2)}, u32[]{:S(2)}) collective-permute-start(bf16[3,336,512]{2,1,0:T(8,128)(2,1)} %fusion.1), channel_id=1, source_target_pairs={{0,2},{1,3},{2,0},{3,1},{4,6},{5,7},{6,4},{7,5},{8,10},{9,11},{10,... | collective-permute-start | bytes 3096584 | tf_op jit(solution)/shard_map/ppermute | solution.py:980
  160.7 23.5 %collective-permute-start.11 = (bf16[2,3,336,128]{3,2,1,0:T(8,128)(2,1)}, bf16[2,3,336,128]{3,2,1,0:T(8,128)(2,1)}, u32[]{:S(2)}, u32[]{:S(2)}) collective-permute-start(bf16[2,3,336,128]{3,2,1,0:T(8,128)(2,1)} %get-tuple-element.60), channel_id=1, source_target_pairs={{0,3},{1,2},{2,1},{3,0},{4,7},{5,6},{6,5},{7,4},{8,11},{9,10},{10,... | collective-permute-start | bytes 1548296 | tf_op jit(solution)/shard_map/ppermute | solution.py:980
  241.8 25.5 %collective-permute-start.45 = (bf16[5136,128]{1,0:T(8,128)(2,1)}, bf16[5136,128]{1,0:T(8,128)(2,1)S(1)}, u32[]{:S(2)}, u32[]{:S(2)}) collective-permute-start(bf16[5136,128]{1,0:T(8,128)(2,1)} %get-tuple-element.94), channel_id=1, source_target_pairs={{0,1},{1,0},{2,3},{3,2},{4,5},{5,4},{6,7},{7,6},{8,9},{9,8},{10,11... | collective-permute-start | bytes 3944456 | tf_op jit(solution)/shard_map/ppermute | solution.py:980
  241.9 25.4 %collective-permute-start.16 = (bf16[3,336,512]{2,1,0:T(8,128)(2,1)}, bf16[3,336,512]{2,1,0:T(8,128)(2,1)S(1)}, u32[]{:S(2)}, u32[]{:S(2)}) collective-permute-start(bf16[3,336,512]{2,1,0:T(8,128)(2,1)} %get-tuple-element.62), channel_id=1, source_target_pairs={{0,2},{1,3},{2,0},{3,1},{4,6},{5,7},{6,4},{7,5},{8,10},{9,11},{10,... | collective-permute-start | bytes 3096584 | tf_op jit(solution)/shard_map/ppermute | solution.py:980
  243.4 31.3 %collective-permute-start.15 = (bf16[3,336,512]{2,1,0:T(8,128)(2,1)}, bf16[3,336,512]{2,1,0:T(8,128)(2,1)S(1)}, u32[]{:S(2)}, u32[]{:S(2)}) collective-permute-start(bf16[3,336,512]{2,1,0:T(8,128)(2,1)} %get-tuple-element.62), channel_id=1, source_target_pairs={{0,1},{1,0},{2,3},{3,2},{4,5},{5,4},{6,7},{7,6},{8,9},{9,8},{10,11... | collective-permute-start | bytes 3096584 | tf_op jit(solution)/shard_map/ppermute | solution.py:980
  243.6 37.4 %collective-permute-start.44 = (bf16[5136,128]{1,0:T(8,128)(2,1)}, bf16[5136,128]{1,0:T(8,128)(2,1)}, u32[]{:S(2)}, u32[]{:S(2)}) collective-permute-start(bf16[5136,128]{1,0:T(8,128)(2,1)} %get-tuple-element.92), channel_id=1, source_target_pairs={{0,1},{1,0},{2,3},{3,2},{4,5},{5,4},{6,7},{7,6},{8,9},{9,8},{10,11... | collective-permute-start | bytes 3944456 | tf_op jit(solution)/shard_map/ppermute | solution.py:980
  270.4 31.2 %collective-permute-start.46 = (bf16[5136,128]{1,0:T(8,128)(2,1)}, bf16[5136,128]{1,0:T(8,128)(2,1)}, u32[]{:S(2)}, u32[]{:S(2)}) collective-permute-start(bf16[5136,128]{1,0:T(8,128)(2,1)} %add_convert_fusion.1), channel_id=1, source_target_pairs={{0,2},{1,3},{2,0},{3,1},{4,6},{5,7},{6,4},{7,5},{8,10},{9,11},{10,... | collective-permute-start | bytes 3944456 | tf_op jit(solution)/shard_map/ppermute | solution.py:980
  304.9 246.5 %reduce-scatter.2.cloned.1.call-start = ((), (), s32[]{:S(2)}) async-start(), calls=%async_computation.3 | async-start | bytes 4128768 | tf_op jit(solution)/shard_map/reduce_scatter | solution.py:1125
  306.6 23.4 %collective-permute-start.20 = (bf16[2,3,336,128]{3,2,1,0:T(8,128)(2,1)S(1)}, bf16[2,3,336,128]{3,2,1,0:T(8,128)(2,1)S(1)}, u32[]{:S(2)}, u32[]{:S(2)}) collective-permute-start(bf16[2,3,336,128]{3,2,1,0:T(8,128)(2,1)S(1)} %copy-done.38), channel_id=1, source_target_pairs={{0,3},{1,2},{2,1},{3,0},{4,7},{5,6},{6,5},{7,4},{8,11},{9,10},{10,... | collective-permute-start | bytes 1548296 | tf_op jit(solution)/shard_map/ppermute | solution.py:980
  380.9 20.4 %collective-permute-start.43 = (bf16[640,128]{1,0:T(8,128)(2,1)}, bf16[640,128]{1,0:T(8,128)(2,1)}, u32[]{:S(2)}, u32[]{:S(2)}) collective-permute-start(bf16[640,128]{1,0:T(8,128)(2,1)} %get-tuple-element.90.refs_0_), channel_id=1, source_target_pairs={{0,28},{4,24},{8,20},{12,16},{16,12},{20,8},{24,4},{28,0},{1,29},{... | collective-permute-start | bytes 491528 | tf_op jit(solution)/shard_map/ppermute | solution.py:980
  383.2 22.2 %collective-permute-start.42 = (bf16[640,128]{1,0:T(8,128)(2,1)}, bf16[640,128]{1,0:T(8,128)(2,1)}, u32[]{:S(2)}, u32[]{:S(2)}) collective-permute-start(bf16[640,128]{1,0:T(8,128)(2,1)} %get-tuple-element.90.refs_0_), channel_id=1, source_target_pairs={{0,24},{4,28},{8,16},{12,20},{16,8},{20,12},{24,0},{28,4},{1,25},{... | collective-permute-start | bytes 491528 | tf_op jit(solution)/shard_map/ppermute | solution.py:980
  386.9 40.9 %collective-permute-start.41 = (bf16[640,128]{1,0:T(8,128)(2,1)}, bf16[640,128]{1,0:T(8,128)(2,1)}, u32[]{:S(2)}, u32[]{:S(2)}) collective-permute-start(bf16[640,128]{1,0:T(8,128)(2,1)} %get-tuple-element.90.refs_0_), channel_id=1, source_target_pairs={{0,20},{4,16},{8,28},{12,24},{16,4},{20,0},{24,12},{28,8},{1,21},{... | collective-permute-start | bytes 491528 | tf_op jit(solution)/shard_map/ppermute | solution.py:980
  386.9 52.9 %collective-permute-start.40 = (bf16[640,128]{1,0:T(8,128)(2,1)}, bf16[640,128]{1,0:T(8,128)(2,1)}, u32[]{:S(2)}, u32[]{:S(2)}) collective-permute-start(bf16[640,128]{1,0:T(8,128)(2,1)} %get-tuple-element.90.refs_0_), channel_id=1, source_target_pairs={{0,16},{4,20},{8,24},{12,28},{16,0},{20,4},{24,8},{28,12},{1,17},{... | collective-permute-start | bytes 491528 | tf_op jit(solution)/shard_map/ppermute | solution.py:980
  389.9 52.5 %collective-permute-start.39 = (bf16[640,128]{1,0:T(8,128)(2,1)}, bf16[640,128]{1,0:T(8,128)(2,1)}, u32[]{:S(2)}, u32[]{:S(2)}) collective-permute-start(bf16[640,128]{1,0:T(8,128)(2,1)} %get-tuple-element.90.refs_0_), channel_id=1, source_target_pairs={{0,12},{4,8},{8,4},{12,0},{16,28},{20,24},{24,20},{28,16},{1,13},{... | collective-permute-start | bytes 491528 | tf_op jit(solution)/shard_map/ppermute | solution.py:980
  401.3 41.2 %collective-permute-start.38 = (bf16[640,128]{1,0:T(8,128)(2,1)}, bf16[640,128]{1,0:T(8,128)(2,1)}, u32[]{:S(2)}, u32[]{:S(2)}) collective-permute-start(bf16[640,128]{1,0:T(8,128)(2,1)} %get-tuple-element.90.refs_0_), channel_id=1, source_target_pairs={{0,8},{4,12},{8,0},{12,4},{16,24},{20,28},{24,16},{28,20},{1,9},{5... | collective-permute-start | bytes 491528 | tf_op jit(solution)/shard_map/ppermute | solution.py:980
  405.4 39.7 %collective-permute-start.37 = (bf16[640,128]{1,0:T(8,128)(2,1)}, bf16[640,128]{1,0:T(8,128)(2,1)}, u32[]{:S(2)}, u32[]{:S(2)}) collective-permute-start(bf16[640,128]{1,0:T(8,128)(2,1)} %get-tuple-element.90.refs_0_), channel_id=1, source_target_pairs={{0,4},{4,0},{8,12},{12,8},{16,20},{20,16},{24,28},{28,24},{1,5},{5... | collective-permute-start | bytes 491528 | tf_op jit(solution)/shard_map/ppermute | solution.py:980
  427.9 41.4 %collective-permute-start.36 = (bf16[624,128]{1,0:T(8,128)(2,1)}, bf16[624,128]{1,0:T(8,128)(2,1)}, u32[]{:S(2)}, u32[]{:S(2)}) collective-permute-start(bf16[624,128]{1,0:T(8,128)(2,1)} %bitcast.108), channel_id=1, source_target_pairs={{0,28},{4,24},{8,20},{12,16},{16,12},{20,8},{24,4},{28,0},{1,29},{... | collective-permute-start | bytes 479240 | tf_op jit(solution)/shard_map/ppermute | solution.py:980
  439.8 29.5 %collective-permute-start.35 = (bf16[624,128]{1,0:T(8,128)(2,1)}, bf16[624,128]{1,0:T(8,128)(2,1)}, u32[]{:S(2)}, u32[]{:S(2)}) collective-permute-start(bf16[624,128]{1,0:T(8,128)(2,1)} %bitcast.109), channel_id=1, source_target_pairs={{0,24},{4,28},{8,16},{12,20},{16,8},{20,12},{24,0},{28,4},{1,25},{... | collective-permute-start | bytes 479240 | tf_op jit(solution)/shard_map/ppermute | solution.py:980
  442.5 32.4 %collective-permute-start.34 = (bf16[624,128]{1,0:T(8,128)(2,1)}, bf16[624,128]{1,0:T(8,128)(2,1)}, u32[]{:S(2)}, u32[]{:S(2)}) collective-permute-start(bf16[624,128]{1,0:T(8,128)(2,1)} %bitcast.110), channel_id=1, source_target_pairs={{0,20},{4,16},{8,28},{12,24},{16,4},{20,0},{24,12},{28,8},{1,21},{... | collective-permute-start | bytes 479240 | tf_op jit(solution)/shard_map/ppermute | solution.py:980
  442.5 39.5 %collective-permute-start.33 = (bf16[624,128]{1,0:T(8,128)(2,1)}, bf16[624,128]{1,0:T(8,128)(2,1)}, u32[]{:S(2)}, u32[]{:S(2)}) collective-permute-start(bf16[624,128]{1,0:T(8,128)(2,1)} %bitcast.111), channel_id=1, source_target_pairs={{0,16},{4,20},{8,24},{12,28},{16,0},{20,4},{24,8},{28,12},{1,17},{... | collective-permute-start | bytes 479240 | tf_op jit(solution)/shard_map/ppermute | solution.py:980
  445.1 65.3 %collective-permute-start.28 = (bf16[3,336,512]{2,1,0:T(8,128)(2,1)}, bf16[3,336,512]{2,1,0:T(8,128)(2,1)}, u32[]{:S(2)}, u32[]{:S(2)}) collective-permute-start(bf16[3,336,512]{2,1,0:T(8,128)(2,1)} %get-tuple-element.85), channel_id=1, source_target_pairs={{0,1},{1,0},{2,3},{3,2},{4,5},{5,4},{6,7},{7,6},{8,9},{9,8},{10,11... | collective-permute-start | bytes 3096584 | tf_op jit(solution)/shard_map/ppermute | solution.py:980
  469.2 21.7 %collective-permute-start.32 = (bf16[624,128]{1,0:T(8,128)(2,1)}, bf16[624,128]{1,0:T(8,128)(2,1)}, u32[]{:S(2)}, u32[]{:S(2)}) collective-permute-start(bf16[624,128]{1,0:T(8,128)(2,1)} %bitcast.112), channel_id=1, source_target_pairs={{0,12},{4,8},{8,4},{12,0},{16,28},{20,24},{24,20},{28,16},{1,13},{... | collective-permute-start | bytes 479240 | tf_op jit(solution)/shard_map/ppermute | solution.py:980
  469.3 29.4 %collective-permute-start.31 = (bf16[624,128]{1,0:T(8,128)(2,1)}, bf16[624,128]{1,0:T(8,128)(2,1)}, u32[]{:S(2)}, u32[]{:S(2)}) collective-permute-start(bf16[624,128]{1,0:T(8,128)(2,1)} %bitcast.113), channel_id=1, source_target_pairs={{0,8},{4,12},{8,0},{12,4},{16,24},{20,28},{24,16},{28,20},{1,9},{5... | collective-permute-start | bytes 479240 | tf_op jit(solution)/shard_map/ppermute | solution.py:980
  474.9 23.8 %collective-permute-start.30 = (bf16[624,128]{1,0:T(8,128)(2,1)}, bf16[624,128]{1,0:T(8,128)(2,1)}, u32[]{:S(2)}, u32[]{:S(2)}) collective-permute-start(bf16[624,128]{1,0:T(8,128)(2,1)} %bitcast.114), channel_id=1, source_target_pairs={{0,4},{4,0},{8,12},{12,8},{16,20},{20,16},{24,28},{28,24},{1,5},{5... | collective-permute-start | bytes 479240 | tf_op jit(solution)/shard_map/ppermute | solution.py:980
  482.0 36.1 %collective-permute-start.27 = (bf16[3,336,512]{2,1,0:T(8,128)(2,1)}, bf16[3,336,512]{2,1,0:T(8,128)(2,1)}, u32[]{:S(2)}, u32[]{:S(2)}) collective-permute-start(bf16[3,336,512]{2,1,0:T(8,128)(2,1)} %get-tuple-element.83), channel_id=1, source_target_pairs={{0,1},{1,0},{2,3},{3,2},{4,5},{5,4},{6,7},{7,6},{8,9},{9,8},{10,11... | collective-permute-start | bytes 3096584 | tf_op jit(solution)/shard_map/ppermute | solution.py:980
  512.3 24.8 %collective-permute-start.29 = (bf16[3,336,512]{2,1,0:T(8,128)(2,1)S(1)}, bf16[3,336,512]{2,1,0:T(8,128)(2,1)S(1)}, u32[]{:S(2)}, u32[]{:S(2)}) collective-permute-start(bf16[3,336,512]{2,1,0:T(8,128)(2,1)S(1)} %add_convert_fusion.3), channel_id=1, source_target_pairs={{0,2},{1,3},{2,0},{3,1},{4,6},{5,7},{6,4},{7,5},{8,10},{9,11},{10,... | collective-permute-start | bytes 3096584 | tf_op jit(solution)/shard_map/ppermute | solution.py:980
  (65 other events, 446.2 us)
Sparse Core Ops, SparseCore 0:
  13.9 79.2 all-gather.2
  305.1 135.5 all-reduce.3
  444.8 96.5 reduce-scatter.1
